TPU v7x, 512 devices: a whole 4x4x16 slice. The times are simulated.
512 devices in a mesh: pts: 128 (over y, z, core), ch: 4 (over x).
Axes of the slice: x: 4, y: 4, z: 16, core: 2. Of those that a mesh axis runs over, the one named last changes fastest.
Arguments:
- raw_points: bfloat16 [393216, 128], P('pts'), may hold values from -36 to 36
- cell_ids: int32 [393216], P('pts'), may hold values from 0 to 2047, as said below
- row_counts: int32 [128], replicated, may hold values from 512 to 2048, as said below
- hilbert_position: int32 [128, 2048], P('pts'), may hold values from -1 to 131071, as said below
- z_position: int32 [131072], P('pts'), may hold values from 0 to 131071, as said below
- pool_weight: bfloat16 [128, 256], replicated, may hold values from -0.5 to 0.5
- qkv_weight: bfloat16 [3, 256, 256], P(None, None, 'ch')
- proj_weight: bfloat16 [256, 256], P(None, 'ch'), may hold values from -0.375 to 0.375
- fc1_weight: bfloat16 [256, 1024], P(None, 'ch'), may hold values from -0.375 to 0.375
- fc2_weight: bfloat16 [1024, 256], P('ch'), may hold values from -0.1875 to 0.1875
Outputs:
- returned: bfloat16 [131072, 256], P('pts', 'ch')
Inputs may be any that keep to these rules, and one draw needn't show every extreme that they name: `row_counts`: each count is a multiple of 128; the counts sum to 131072; the largest is 2048 and the smallest is 512. `cell_ids`: on each device the ids never fall, start at 0, skip no id and end at that device's count minus 1. `hilbert_position`: entry l of device a is -1 exactly where l >= row_counts[a]; the other entries together are a permutation of the 131072 positions; device a's cells go to each device's block of 1024 Hilbert positions in equal numbers, row_counts[a] / 128. `z_position`: the inverse of the placement given by hilbert_position; each block of 1024 Hilbert positions sends exactly 8 of its cells to each block of 1024 Z indices.
All inputs are finite; a program needn't handle non-finite values.
Results may differ from a plain program's by a relative error of at most 0.014.
The roundings to bfloat16 on the way count: a program that leaves them out, or rounds other values in their place, can miss the bound.
Values may be sent and summed in bfloat16 or wider, within the bound.
A program may use at most 64 MiB of HBM per device.

v0:
```python
from functools import partial

import jax
import jax.numpy as jnp
from jax import lax
from jax.sharding import PartitionSpec as P

HEADS = 16
PATCH = 1024


eps_norm = 1e-05


def layer_norm(values):
    values = values.astype(jnp.float32)
    center = values - jnp.mean(values, axis=-1, keepdims=True)
    spread = jnp.mean(center * center, axis=-1, keepdims=True)
    return center * lax.rsqrt(spread + eps_norm)


def slot_table(target_dev, is_live, peer_count, slot_width):
    item_count = target_dev.shape[0]
    keyed = jnp.where(is_live, target_dev, peer_count)
    ranking = jnp.argsort(keyed, stable=True)
    ranked = keyed[ranking]
    starts = jnp.searchsorted(ranked, jnp.arange(peer_count + 1, dtype=jnp.int32))
    slot_place = jnp.arange(item_count, dtype=jnp.int32) - starts[ranked]
    slot_index = jnp.where(
        ranked < peer_count, ranked * slot_width + slot_place, peer_count * slot_width
    )
    return (ranking, slot_index)


def fill_slots(values, ranking, slot_index, total, blank):
    padded = jnp.full((total + 1,) + values.shape[1:], blank, values.dtype)
    return padded.at[slot_index].set(values[ranking])[:total]


def settle(values, positions, first_row, row_count):
    flat = values.reshape(-1, values.shape[-1])
    spots = positions.reshape(-1).astype(jnp.int32)
    spots = jnp.where(spots >= 0, spots - first_row, row_count)
    holder = jnp.zeros((row_count + 1, flat.shape[1]), values.dtype)
    return holder.at[spots].set(flat)[:row_count]


def attend_item(score_scale, blocks):
    query_blk, key_blk, value_blk = blocks
    scores = (
        jnp.einsum("qd,kd->qk", query_blk, key_blk, preferred_element_type=jnp.float32)
        * score_scale
    )
    peak = jnp.max(scores, axis=-1, keepdims=True)
    raised = jnp.exp(scores - peak)
    weights = (raised / jnp.sum(raised, axis=-1, keepdims=True)).astype(jnp.bfloat16)
    return jnp.dot(weights, value_blk, preferred_element_type=jnp.float32).astype(jnp.bfloat16)


def shards(
    raw_points,
    cell_ids,
    row_counts,
    hilbert_position,
    z_position,
    pool_weight,
    qkv_weight,
    proj_weight,
    fc1_weight,
    fc2_weight,
):
    peer_count = lax.axis_size("pts")
    row_count = z_position.shape[0]
    cell_limit = hilbert_position.shape[1]
    slot_width = cell_limit // peer_count
    back_width = row_count // peer_count
    first_row = lax.axis_index("pts") * row_count
    ch_index = lax.axis_index("ch")
    full_width = proj_weight.shape[0]
    own_width = proj_weight.shape[1]
    in_width = raw_points.shape[1]
    cell_sums = jax.ops.segment_sum(
        raw_points.astype(jnp.float32), cell_ids, num_segments=cell_limit
    )
    cell_tally = jax.ops.segment_sum(
        jnp.ones(cell_ids.shape, jnp.float32), cell_ids, num_segments=cell_limit
    )
    pooled = (cell_sums / jnp.maximum(cell_tally, 1.0)[:, None]).astype(jnp.bfloat16)
    target_row = hilbert_position[0]
    is_live = target_row >= 0
    ranking, slot_index = slot_table(
        jnp.where(is_live, target_row // row_count, 0), is_live, peer_count, slot_width
    )
    total = peer_count * slot_width
    slot_rows = fill_slots(target_row, ranking, slot_index, total, -1).reshape(
        peer_count, slot_width
    )
    outgoing = fill_slots(pooled, ranking, slot_index, total, 0).reshape(
        peer_count, slot_width, in_width
    )
    rows_in = lax.all_to_all(outgoing, "pts", split_axis=0, concat_axis=0, tiled=True)
    positions = lax.all_to_all(slot_rows, "pts", split_axis=0, concat_axis=0, tiled=True)
    projected = jnp.einsum("pwc,cd->pwd", rows_in, pool_weight, preferred_element_type=jnp.float32)
    arrived = projected.astype(jnp.bfloat16)
    features = settle(arrived, positions, first_row, row_count)
    own_features = lax.dynamic_slice_in_dim(features, ch_index * own_width, own_width, 1)
    normed = layer_norm(features).astype(jnp.bfloat16)
    qkv_rows = jnp.einsum(
        "rc,kcd->krd", normed, qkv_weight, preferred_element_type=jnp.float32
    ).astype(jnp.bfloat16)
    head_dim = full_width // HEADS
    local_heads = own_width // head_dim
    patch_count = row_count // PATCH
    grouped = qkv_rows.reshape(3, patch_count, PATCH, local_heads, head_dim).transpose(
        0, 1, 3, 2, 4
    )
    grouped = grouped.reshape(3, patch_count * local_heads, PATCH, head_dim)
    attended = lax.map(
        partial(attend_item, head_dim ** (-0.5)), (grouped[0], grouped[1], grouped[2])
    )
    attended = (
        attended.reshape(patch_count, local_heads, PATCH, head_dim)
        .transpose(0, 2, 1, 3)
        .reshape(row_count, own_width)
    )
    mixture = jnp.dot(
        lax.all_gather(attended, "ch", axis=1, tiled=True),
        proj_weight,
        preferred_element_type=jnp.float32,
    )
    block_mid = (own_features.astype(jnp.float32) + mixture).astype(jnp.bfloat16)
    whole_mid = lax.all_gather(block_mid, "ch", axis=1, tiled=True)
    normed2 = layer_norm(whole_mid).astype(jnp.bfloat16)
    hidden = jax.nn.gelu(
        jnp.dot(normed2, fc1_weight, preferred_element_type=jnp.float32), approximate=False
    ).astype(jnp.bfloat16)
    partial_sums = jnp.dot(hidden, fc2_weight, preferred_element_type=jnp.float32)
    summed = lax.psum_scatter(
        partial_sums.astype(jnp.bfloat16), "ch", scatter_dimension=1, tiled=True
    ).astype(jnp.float32)
    result = (block_mid.astype(jnp.float32) + summed).astype(jnp.bfloat16)
    back_ranking, back_index = slot_table(
        z_position // row_count, z_position >= 0, peer_count, back_width
    )
    back_total = peer_count * back_width
    outgoing_rows = fill_slots(result, back_ranking, back_index, back_total, 0).reshape(
        peer_count, back_width, own_width
    )
    outgoing_at = fill_slots(z_position, back_ranking, back_index, back_total, -1).reshape(
        peer_count, back_width
    )
    returned_rows, returned_at = (
        lax.all_to_all(outgoing_rows, "pts", split_axis=0, concat_axis=0, tiled=True),
        lax.all_to_all(outgoing_at, "pts", split_axis=0, concat_axis=0, tiled=True),
    )
    return settle(returned_rows, returned_at, first_row, row_count)


def solution(mesh):
    in_specs = (
        P("pts", None),
        P("pts"),
        P(),
        P("pts", None),
        P("pts"),
        P(),
        P(None, None, "ch"),
        P(None, "ch"),
        P(None, "ch"),
        P("ch", None),
    )
    out_specs = P("pts", "ch")
    return jax.shard_map(shards, mesh=mesh, in_specs=in_specs, out_specs=out_specs, check_vma=False)
```

profile of v0, /device:TPU:6, one launch (start us, length us, event | category | flops | bytes accessed | tf_op | source)
XLA Modules:
  0.0 343.3 jit_solution(13302240868907910295)
XLA Ops:
  7.3 5.0 %sort.35 = (s32[2048]{0:T(1024)}, s32[2048]{0:T(1024)S(1)}) sort(s32[2048]{0:T(1024)S(1)} %select_select_fusion, s32[2048]{0:T(1024)S(1)} %iota.25), dimensions={0}, to_apply=%region_4.5 | sort | flops 22528 | bytes 32768 | tf_op jit(solution)/shard_map/jit(argsort)/sort | solution.py:25
  12.3 11.8 %gather_fusion.5 = s32[2048]{0:T(1024)S(1)} fusion(s32[2048]{0:T(1024)S(1)} %select_select_fusion, s32[2048]{0:T(1024)S(1)} %fusion.105), kind=kCustom, calls=%fused_computation.5 | custom fusion | bytes 24576 | tf_op jit(solution)/shard_map/gather | solution.py:26
  24.1 11.8 %gather_fusion.7 = s32[2048]{0:T(1024)S(1)} fusion(s32[2048]{0:T(1024)S(1)} %bitcast.76, s32[2048]{0:T(1024)S(1)} %fusion.105), kind=kCustom, calls=%fused_computation.7 | custom fusion | bytes 24576 | tf_op jit(solution)/shard_map/gather | solution.py:37
  35.9 18.1 %while.60 = (s32[]{:T(128)}, u32[129]{0:T(256)S(1)}, u32[129]{0:T(256)S(1)}, s32[2048]{0:T(1024)S(1)}, s32[]{:T(128)}, /*index=5*/s32[]{:T(128)}, s32[]{}) while((s32[]{:T(128)}, u32[129]{0:T(256)S(1)}, u32[129]{0:T(256)S(1)}, s32[2048]{0:T(1024)S(1)}, s32[]{:T(128)}, /*index=5*/s32[]{:T(128)}, s32[]{}) %tuple.82), condition=%wide.region_6.7_spmd.clone, body=%wide.region_5.6_spmd.clone.sunk | while | flops 2705 | bytes 10388 | solution.py:27
  36.0 1.4 gather_fusion.1
  37.5 1.4 gather_fusion.1
  39.0 1.4 gather_fusion.1
  40.5 1.4 gather_fusion.1
  42.0 1.4 gather_fusion.1
  43.5 1.4 gather_fusion.1
  45.0 1.4 gather_fusion.1
  46.6 1.4 gather_fusion.1
  48.1 1.4 gather_fusion.1
  49.6 1.4 gather_fusion.1
  51.1 1.4 gather_fusion.1
  52.6 1.4 gather_fusion.1
  54.1 13.1 %gather_fusion.6 = s32[2048]{0:T(1024)S(1)} fusion(s32[129]{0:T(256)S(1)} %convert_element_type.74, s32[2048]{0:T(1024)S(1)} %broadcast_clamp_fusion), kind=kCustom, calls=%fused_computation.6 | custom fusion | bytes 24576 | tf_op jit(solution)/shard_map/gather | solution.py:28
  67.3 8.1 %scatter_custom_fusion.1 = s32[2049]{0:T(1024)S(1)} fusion(s32[2048]{0:T(1024)S(1)} %bitcast.90, s32[2048]{0:T(1024)S(1)} %gather_fusion.7, s32[]{:T(128)} %constant.85.clone.1), kind=kCustom, calls=%fused_computation.168 | custom fusion | bytes 8200 | tf_op jit(solution)/shard_map/scatter | solution.py:37
  76.1 20.0 %all-to-all-start.1 = ((s32[128,1,16]{2,1,0:T(1,128)}), s32[128,1,16]{2,1,0:T(1,128)S(1)}, u32[]{:S(2)}, u32[]{:S(2)}) async-start(s32[128,1,16]{2,1,0:T(1,128)} %bitcast.15), calls=%async_computation.1 | async-start | bytes 131072 | tf_op jit(solution)/shard_map/all_to_all | solution.py:102
  96.0 18.6 %scatter_custom_fusion.2 = f32[2048,128]{1,0:T(8,128)S(1)} fusion(s32[3072]{0:T(1024)} %param.17, bf16[3072,128]{1,0:T(8,128)(2,1)S(1)} %copy-done.3, f32[]{:T(128)} %constant.183.clone.1), kind=kCustom, calls=%fused_computation.53 | custom fusion | flops 786432 | bytes 1835520 | tf_op jit(solution)/shard_map/scatter-add | solution.py:82
  114.6 22.3 %scatter_custom_fusion.3 = f32[2048]{0:T(1024)S(1)} fusion(s32[3072]{0:T(1024)} %param.17, f32[3072]{0:T(1024)S(1)} %broadcast.284, f32[]{:T(128)} %constant.183.clone.1), kind=kCustom, calls=%fused_computation.181 | custom fusion | flops 3072 | bytes 8704 | tf_op jit(solution)/shard_map/scatter-add | solution.py:85
  137.4 12.0 %scatter_custom_fusion.4 = bf16[2049,128]{1,0:T(8,128)(2,1)S(1)} fusion(s32[2048]{0:T(1024)S(1)} %bitcast.91, bf16[2048,128]{1,0:T(8,128)(2,1)S(1)} %divide_convert_fusion.8, s32[2048]{0:T(1024)S(1)} %fusion.105, bf16[]{:T(256)} %constant.84.clone.1), kind=kCustom, calls=%fused_computation.93 | custom fusion | bytes 524546 | tf_op jit(solution)/shard_map/scatter | solution.py:37
  149.4 0.8 slice.61
  150.2 16.2 %all-to-all-start.2 = ((bf16[128,16,128]{2,1,0:T(8,128)(2,1)}), bf16[128,16,128]{2,1,0:T(8,128)(2,1)S(1)}, u32[]{:S(2)}, u32[]{:S(2)}) async-start(bf16[128,16,128]{2,1,0:T(8,128)(2,1)} %bitcast.17), calls=%async_computation.2 | async-start | bytes 1048576 | tf_op jit(solution)/shard_map/all_to_all | solution.py:101
  166.5 4.4 %sort.34 = (s32[1024]{0:T(1024)}, s32[1024]{0:T(1024)S(1)}) sort(s32[1024]{0:T(1024)S(1)} %fusion.110, s32[1024]{0:T(1024)S(1)} %iota.22), dimensions={0}, to_apply=%region_0.0 | sort | flops 10240 | bytes 16384 | tf_op jit(solution)/shard_map/jit(argsort)/sort | solution.py:25
  170.9 4.5 %gather_fusion.2 = s32[1024]{0:T(1024)S(1)} fusion(s32[1024]{0:T(1024)S(1)} %fusion.110, s32[1024]{0:T(1024)S(1)} %fusion.111), kind=kCustom, calls=%fused_computation.2 | custom fusion | bytes 12288 | tf_op jit(solution)/shard_map/gather | solution.py:26
  175.8 24.1 %all-to-all-done.2 = bf16[128,16,128]{2,1,0:T(8,128)(2,1)S(1)} async-done(((bf16[128,16,128]{2,1,0:T(8,128)(2,1)}), bf16[128,16,128]{2,1,0:T(8,128)(2,1)S(1)}, u32[]{:S(2)}, u32[]{:S(2)}) %all-to-all-start.2) | async-done | bytes 524320 | tf_op jit(solution)/shard_map/all_to_all | solution.py:101
  201.0 9.5 %scatter_custom_fusion.5 = bf16[1025,256]{1,0:T(8,128)(2,1)S(1)} fusion(s32[2048]{0:T(1024)S(1)} %bitcast.92, bf16[2048,256]{1,0:T(8,128)(2,1)S(1)} %bitcast.83, bf16[]{:T(256)} %constant.84.clone.1), kind=kCustom, calls=%fused_computation.130 | custom fusion | bytes 524802 | tf_op jit(solution)/shard_map/scatter | solution.py:45
  211.4 9.5 %while.58 = (s32[]{:T(128)}, bf16[4,1024,16]{1,2,0:T(8,128)(2,1)S(1)}, bf16[4,1024,16]{1,2,0:T(8,128)(2,1)S(1)}, bf16[4,1024,16]{1,2,0:T(8,128)(2,1)S(1)}, bf16[4,1024,16]{1,2,0:T(8,128)(2,1)S(1)}, /*index=5*/s32[]{:T(128)}) while((s32[]{:T(128)}, bf16[4,1024,16]{1,2,0:T(8,128)(2,1)S(1)}, bf16[4,1024,16]{1,2,0:T(8,128)(2,1)S(1)}, ...), condition=%wide.region_17.18_spmd, body=%wide.region_14.17_spmd.sunk | while | flops 76560384 | bytes 12736581 | solution.py:118
  211.5 0.8 multiply_reduce_fusion.2
  213.0 0.9 fusion.159
  213.8 0.8 multiply_reduce_fusion.2
  215.3 0.9 fusion.159
  216.2 0.8 multiply_reduce_fusion.2
  217.7 0.9 fusion.159
  218.6 0.8 multiply_reduce_fusion.2
  220.1 0.9 fusion.159
  220.9 13.5 %all_gather.6 = bf16[1024,256]{0,1:T(8,128)(2,1)S(1)} all-gather(bf16[1024,64]{0,1:T(8,128)(2,1)S(1)} %bitcast.84), channel_id=1, replica_groups=mesh['pts'=128,'ch'=4] {'ch'}, dimensions={1}, use_global_device_ids=true | all-gather | bytes 655360 | tf_op jit(solution)/shard_map/all_gather | solution.py:127
  234.6 13.2 %all_gather.7 = bf16[1024,256]{0,1:T(8,128)(2,1)S(1)} all-gather(bf16[1024,64]{0,1:T(8,128)(2,1)S(1)} %fusion.29), channel_id=1, replica_groups=mesh['pts'=128,'ch'=4] {'ch'}, dimensions={1}, use_global_device_ids=true | all-gather | bytes 655360 | tf_op jit(solution)/shard_map/all_gather | solution.py:132
  248.1 3.6 %convolution_convert_fusion.1 = bf16[1024,256]{0,1:T(8,128)(2,1)} fusion(bf16[256,256]{1,0:T(8,128)(2,1)S(1)} %copy-done, bf16[256,256]{1,0:T(8,128)(2,1)S(1)} %copy-done.7, bf16[1024,256]{0,1:T(8,128)(2,1)S(1)} %all_gather.7, f32[1024]{0:T(1024)S(1)} %add_rsqrt_fusion, f32[1024]{0:T(1024)S(1)} %broadcast_multiply_fusion), kind=kOutput, calls=%fused_computation.60 | convolution fusion | flops 286785536 | bytes 1318912 | tf_op jit(solution)/shard_map/dot_general | solution.py:137
  251.7 13.7 %while.59 = (s32[]{:T(128)}, u32[129]{0:T(256)S(1)}, u32[129]{0:T(256)S(1)}, s32[1024]{0:T(1024)S(1)}, s32[]{:T(128)}, /*index=5*/s32[]{:T(128)}, s32[]{}) while((s32[]{:T(128)}, u32[129]{0:T(256)S(1)}, u32[129]{0:T(256)S(1)}, s32[1024]{0:T(1024)S(1)}, s32[]{:T(128)}, /*index=5*/s32[]{:T(128)}, s32[]{}) %tuple.79), condition=%wide.region_2.3_spmd.clone, body=%wide.region_1.0_spmd.clone.sunk | while | flops 2705 | bytes 10388 | solution.py:27
  251.7 1.2 gather_fusion
  253.0 1.2 gather_fusion
  254.2 1.2 gather_fusion
  255.4 1.2 gather_fusion
  256.7 1.2 gather_fusion
  257.9 1.2 gather_fusion
  259.2 1.2 gather_fusion
  260.4 1.2 gather_fusion
  261.6 1.2 gather_fusion
  262.9 1.2 gather_fusion
  264.1 1.2 gather_fusion
  265.3 4.5 %gather_fusion.4 = s32[1024]{0:T(1024)S(1)} fusion(s32[1024]{0:T(1024)S(1)} %copy-done.2, s32[1024]{0:T(1024)S(1)} %fusion.111), kind=kCustom, calls=%fused_computation.4 | custom fusion | bytes 12288 | tf_op jit(solution)/shard_map/gather | solution.py:37
  269.9 6.8 %gather_fusion.3 = s32[1024]{0:T(1024)S(1)} fusion(s32[129]{0:T(256)S(1)} %convert_element_type.73, s32[1024]{0:T(1024)S(1)} %broadcast_clamp_fusion.1), kind=kCustom, calls=%fused_computation.3 | custom fusion | bytes 12288 | tf_op jit(solution)/shard_map/gather | solution.py:28
  276.8 4.3 %scatter_custom_fusion = s32[1025]{0:T(1024)S(1)} fusion(s32[1024]{0:T(1024)S(1)} %bitcast.93, s32[1024]{0:T(1024)S(1)} %gather_fusion.4, s32[]{:T(128)} %constant.85.clone.1), kind=kCustom, calls=%fused_computation.184 | custom fusion | bytes 4104 | tf_op jit(solution)/shard_map/scatter | solution.py:37
  281.8 7.2 %all-to-all-start = ((s32[128,1,8]{2,1,0:T(1,128)}), s32[128,1,8]{2,1,0:T(1,128)S(1)}, u32[]{:S(2)}, u32[]{:S(2)}) async-start(s32[128,1,8]{2,1,0:T(1,128)} %bitcast.8), calls=%async_computation | async-start | bytes 131072 | tf_op jit(solution)/shard_map/all_to_all | solution.py:154
  289.0 0.9 add_convert_fusion
  290.2 6.3 %scatter_custom_fusion.6 = bf16[1025,64]{1,0:T(8,128)(2,1)S(1)} fusion(s32[1024]{0:T(1024)S(1)} %bitcast.94, bf16[1024,64]{1,0:T(8,128)(2,1)S(1)} %copy.27, s32[1024]{0:T(1024)S(1)} %fusion.111, bf16[]{:T(256)} %constant.84.clone.1), kind=kCustom, calls=%fused_computation.136 | custom fusion | bytes 131202 | tf_op jit(solution)/shard_map/scatter | solution.py:37
  296.5 0.9 reshape.445
  297.4 7.3 %all-to-all-done = s32[128,1,8]{2,1,0:T(1,128)S(1)} async-done(((s32[128,1,8]{2,1,0:T(1,128)}), s32[128,1,8]{2,1,0:T(1,128)S(1)}, u32[]{:S(2)}, u32[]{:S(2)}) %all-to-all-start) | async-done | bytes 4128 | tf_op jit(solution)/shard_map/all_to_all | solution.py:154
  304.6 9.0 %all-to-all-start.3 = ((bf16[128,2,256]{2,1,0:T(2,128)(2,1)}), bf16[128,2,256]{2,1,0:T(2,128)(2,1)S(1)}, u32[]{:S(2)}, u32[]{:S(2)}) async-start(bf16[128,2,256]{2,1,0:T(2,128)(2,1)} %reshape.445), calls=%async_computation.4 | async-start | bytes 262144 | tf_op jit(solution)/shard_map/all_to_all | solution.py:153
  314.0 17.9 %all-to-all-done.3 = bf16[128,2,256]{2,1,0:T(2,128)(2,1)S(1)} async-done(((bf16[128,2,256]{2,1,0:T(2,128)(2,1)}), bf16[128,2,256]{2,1,0:T(2,128)(2,1)S(1)}, u32[]{:S(2)}, u32[]{:S(2)}) %all-to-all-start.3) | async-done | bytes 131104 | tf_op jit(solution)/shard_map/all_to_all | solution.py:153
  332.2 3.2 scatter_custom_fusion.7
  335.4 0.8 copy.28
  (145 shorter events, 9.8 us)
Async XLA Ops:
  6.5 241.5 %copy-start = (bf16[256,256]{1,0:T(8,128)(2,1)S(1)}, bf16[256,256]{1,0:T(8,128)(2,1)}, u32[]{:S(2)}) copy-start(bf16[256,256]{1,0:T(8,128)(2,1)} %param.24) | copy-start | bytes 393220
  12.3 11.8 %copy-start.1 = (s32[1,2048]{1,0:T(1,128)S(1)}, s32[1,2048]{1,0:T(1,128)}, u32[]{:S(2)}) copy-start(s32[1,2048]{1,0:T(1,128)} %param.18) | copy-start | bytes 24580
  54.1 42.0 %copy-start.3 = (bf16[3072,128]{1,0:T(8,128)(2,1)S(1)}, bf16[3072,128]{1,0:T(8,128)(2,1)}, u32[]{:S(2)}) copy-start(bf16[3072,128]{1,0:T(8,128)(2,1)} %param.16) | copy-start | bytes 2359300
  67.2 99.3 %copy-start.2 = (s32[1024]{0:T(1024)S(1)}, s32[1024]{0:T(1024)}, u32[]{:S(2)}) copy-start(s32[1024]{0:T(1024)} %param.19) | copy-start | bytes 12292
  76.1 74.1 %all-to-all-start.1 = ((s32[128,1,16]{2,1,0:T(1,128)}), s32[128,1,16]{2,1,0:T(1,128)S(1)}, u32[]{:S(2)}, u32[]{:S(2)}) async-start(s32[128,1,16]{2,1,0:T(1,128)} %bitcast.15), calls=%async_computation.1 | async-start | bytes 131072 | tf_op jit(solution)/shard_map/all_to_all | solution.py:102
  137.0 62.9 %copy-start.5 = (bf16[128,256]{1,0:T(8,128)(2,1)S(1)}, bf16[128,256]{1,0:T(8,128)(2,1)}, u32[]{:S(2)}) copy-start(bf16[128,256]{1,0:T(8,128)(2,1)} %param.20) | copy-start | bytes 196612
  150.2 49.7 %all-to-all-start.2 = ((bf16[128,16,128]{2,1,0:T(8,128)(2,1)}), bf16[128,16,128]{2,1,0:T(8,128)(2,1)S(1)}, u32[]{:S(2)}, u32[]{:S(2)}) async-start(bf16[128,16,128]{2,1,0:T(8,128)(2,1)} %bitcast.17), calls=%async_computation.2 | async-start | bytes 1048576 | tf_op jit(solution)/shard_map/all_to_all | solution.py:101
  166.4 122.6 %reduce-scatter.2.cloned.1.call-start = ((), (), s32[]{:S(2)}) async-start(), calls=%async_computation.5 | async-start | bytes 655360 | tf_op jit(solution)/shard_map/reduce_scatter | solution.py:138
  175.4 35.6 %copy-start.4 = (bf16[3,256,64]{1,2,0:T(8,128)(2,1)S(1)}, bf16[3,256,64]{1,2,0:T(8,128)(2,1)}, u32[]{:S(2)}) copy-start(bf16[3,256,64]{1,2,0:T(8,128)(2,1)} %param.21) | copy-start | bytes 294916
  211.4 23.0 %copy-start.6 = (bf16[256,64]{0,1:T(8,128)(2,1)S(1)}, bf16[256,64]{0,1:T(8,128)(2,1)}, u32[]{:S(2)}) copy-start(bf16[256,64]{0,1:T(8,128)(2,1)} %param.22) | copy-start | bytes 98308
  211.4 36.6 %copy-start.7 = (bf16[256,256]{1,0:T(8,128)(2,1)S(1)}, bf16[256,256]{1,0:T(8,128)(2,1)}, u32[]{:S(2)}) copy-start(bf16[256,256]{1,0:T(8,128)(2,1)} %param.23) | copy-start | bytes 393220
  281.8 22.8 %all-to-all-start = ((s32[128,1,8]{2,1,0:T(1,128)}), s32[128,1,8]{2,1,0:T(1,128)S(1)}, u32[]{:S(2)}, u32[]{:S(2)}) async-start(s32[128,1,8]{2,1,0:T(1,128)} %bitcast.8), calls=%async_computation | async-start | bytes 131072 | tf_op jit(solution)/shard_map/all_to_all | solution.py:154
  304.6 27.3 %all-to-all-start.3 = ((bf16[128,2,256]{2,1,0:T(2,128)(2,1)}), bf16[128,2,256]{2,1,0:T(2,128)(2,1)S(1)}, u32[]{:S(2)}, u32[]{:S(2)}) async-start(bf16[128,2,256]{2,1,0:T(2,128)(2,1)} %reshape.445), calls=%async_computation.4 | async-start | bytes 262144 | tf_op jit(solution)/shard_map/all_to_all | solution.py:153
Sparse Core Ops, SparseCore 0:
  251.8 18.7 reduce-scatter.1
where the time goes:
time: 350 us; the launch traced here: 343 us
  local copies, waits for them, and re-layouts  132 us (38%)
  other arithmetic  57.1 us (16%)
  starting transfers between devices  52.4 us (15%)
  waiting for transfers between devices  49.4 us (14%)
  blocking collectives  26.6 us (8%)
  between operations  14.2 us (4%)
  matrix products  11 us (3%)
    scatter x4, local copies, waits for them, and re-layouts, fill_slots(): return padded.at[slot_index].set(values[ranking])[:total]  30.7 us
    gather x23, local copies, waits for them, and re-layouts, slot_table(): jnp.searchsorted(ranked, jnp.arange(peer_count + 1, dtype=jnp.int32))  30.2 us
    all_to_all x1, waiting for transfers between devices, shards(): lax.all_to_all(outgoing, 'pts', split_axis=0, concat_axis=0, tiled=True)  24.1 us
    scatter-add x1, other arithmetic, shards(): jax.ops.segment_sum(jnp.ones(cell_ids.shape, jnp.float32), cell_ids, num_...  22.3 us
    gather x2, local copies, waits for them, and re-layouts, slot_table(): slot_place = jnp.arange(item_count, dtype=jnp.int32) - starts[ranked]  20 us
    all_to_all x1, starting transfers between devices, shards(): lax.all_to_all(slot_rows, 'pts', split_axis=0, concat_axis=0, tiled=True)  20 us
    scatter-add x1, other arithmetic, shards(): jax.ops.segment_sum(raw_points.astype(jnp.float32), cell_ids, num_segment...  18.6 us
    all_to_all x1, waiting for transfers between devices, shards(): lax.all_to_all(outgoing_rows, 'pts', split_axis=0, concat_axis=0, tiled=T...  17.9 us
  transfers between devices with their start and end apart: 5, of which 3 were waited for; matrix products, arithmetic and copies ran while one was open for 29% of the time, Pallas kernels for 0%

commit v1 on v0

v1 whole, which is shorter than its diff:
```python
import jax
import jax.numpy as jnp
from jax import lax
from jax.experimental import pallas as pl
from jax.experimental.pallas import tpu as pltpu
from jax.sharding import PartitionSpec as P

BF16 = jnp.bfloat16
EPS = 1e-5
MESH = pl.DeviceIdType.MESH
NZ = 16


def place():
    p, c = lax.axis_index("pts"), lax.axis_index("ch")
    return p // 32, lax.rem(p // 2, NZ), lax.rem(p, 2), c


def dev(y, z, k, c):
    return (y * 32 + z * 2 + k, c)


def gather_kernel(slots, pos, pack, rows, posz, wall, mid, s1, r1, s2, r2, s3, r3, ps, pr, ws, wr, fs, fr, loc):
    y, z, k, c = place()
    barrier = pltpu.get_barrier_semaphore()
    off_diag = y != c

    def hello(d):
        pl.semaphore_signal(barrier, inc=1, device_id=d, device_id_type=MESH)

    hello(dev(c, z, 1 - k, y))

    @pl.when(off_diag)
    def _():
        hello(dev(c, z, k, y))
    hello(dev(y, z, 1 - k, c))
    for i in range(1, 4):
        hello(dev(y, z, k, lax.rem(c + i, 4)))

    @pl.loop(1, NZ)
    def _(i):
        hello(dev(y, lax.rem(z + i, NZ), k, c))

    @pl.when(off_diag)
    def _():
        pl.semaphore_wait(barrier, 21)

    @pl.when(jnp.logical_not(off_diag))
    def _():
        pl.semaphore_wait(barrier, 20)

    def stage1(kk):
        return pltpu.make_async_remote_copy(
            src_ref=slots.at[kk], dst_ref=mid.at[:, k], send_sem=s1.at[kk], recv_sem=r1.at[k],
            device_id=dev(c, z, kk, y), device_id_type=MESH)

    def stage1_own():
        return pltpu.make_async_copy(slots.at[k], mid.at[:, k], r1.at[k])

    other = stage1(1 - k)
    other.start()

    @pl.when(off_diag)
    def _():
        stage1(k).start()

    @pl.when(jnp.logical_not(off_diag))
    def _():
        stage1_own().start()

    def pos1(i):
        zz = lax.rem(z + i, NZ)
        return pltpu.make_async_remote_copy(
            src_ref=pos.at[zz], dst_ref=posz.at[z], send_sem=ps.at[i], recv_sem=pr.at[i],
            device_id=dev(y, zz, k, c), device_id_type=MESH)

    own_pos = pltpu.make_async_copy(pos.at[z], posz.at[z], loc.at[0])
    own_pos.start()

    @pl.loop(1, NZ)
    def _(i):
        pos1(i).start()

    HALF = pack.shape[0] // 2
    half = pl.ds(pl.multiple_of(k * HALF, HALF), HALF)
    own_w = pltpu.make_async_copy(pack, wall.at[c], loc.at[1])
    own_w.start()

    def wx(i):
        return pltpu.make_async_remote_copy(
            src_ref=pack.at[half], dst_ref=wall.at[c, half], send_sem=ws.at[i], recv_sem=wr.at[i],
            device_id=dev(y, z, k, lax.rem(c + i, 4)), device_id_type=MESH)
    for i in range(1, 4):
        wx(i).start()

    def mine(kk):
        return pltpu.make_async_copy(slots.at[kk], mid.at[:, kk], r1.at[kk])
    mine(0).wait()
    mine(1).wait()

    def stage2(i):
        zz = lax.rem(z + i, NZ)
        return pltpu.make_async_remote_copy(
            src_ref=mid.at[zz], dst_ref=rows.at[c, z], send_sem=s2.at[i], recv_sem=r2.at[i],
            device_id=dev(y, zz, k, c), device_id_type=MESH)

    @pl.loop(1, NZ)
    def _(i):
        stage2(i).start()
    own = pltpu.make_async_copy(mid.at[z], rows.at[c, z], loc.at[2])
    own.start()
    own.wait()

    def stage3(i, j):
        zs = lax.rem(z - i + NZ, NZ)
        return pltpu.make_async_remote_copy(
            src_ref=rows.at[c, zs], dst_ref=rows.at[c, zs], send_sem=s3.at[i, j], recv_sem=r3.at[i, j],
            device_id=dev(y, z, k, lax.rem(c + j, 4)), device_id_type=MESH)
    for j in range(1, 4):
        stage3(0, j).start()

    @pl.loop(1, NZ)
    def _(i):
        stage2(i).wait_recv()
        for j in range(1, 4):
            stage3(i, j).start()

    own_pos.wait()


    def wf(i):
        src = lax.rem(c - i + 4, 4)
        return pltpu.make_async_remote_copy(
            src_ref=wall.at[src, half], dst_ref=wall.at[src, half], send_sem=fs.at[i], recv_sem=fr.at[i],
            device_id=dev(y, z, 1 - k, c), device_id_type=MESH)
    for i in range(1, 4):
        wx(i).wait_recv()
        wf(i).start()

    own_w.wait()

    @pl.loop(1, NZ)
    def _(i):
        pos1(i).wait()
        stage2(i).wait_send()

    @pl.loop(0, NZ)
    def _(i):
        for j in range(1, 4):
            stage3(i, j).wait()
    for i in range(1, 4):
        wx(i).wait_send()
        wf(i).wait()
    other.wait_send()

    @pl.when(off_diag)
    def _():
        stage1(k).wait_send()


def regroup(slots, pos, pack):
    DMA = pltpu.SemaphoreType.DMA
    any_ = pl.BlockSpec(memory_space=pl.ANY)
    vm = pl.BlockSpec(memory_space=pltpu.VMEM)
    return pl.pallas_call(
        gather_kernel,
        out_shape=(
            jax.ShapeDtypeStruct((4, NZ, 2, 16, 128), jnp.bfloat16),
            jax.ShapeDtypeStruct((NZ, 1, 128), jnp.int32),
            jax.ShapeDtypeStruct((4,) + pack.shape, jnp.bfloat16),
        ),
        in_specs=[vm, vm, any_],
        out_specs=(vm, vm, any_),
        scratch_shapes=[
            pltpu.VMEM((NZ, 2, 16, 128), jnp.bfloat16),
            DMA((2,)), DMA((2,)), DMA((NZ,)), DMA((NZ,)), DMA((NZ, 4)), DMA((NZ, 4)),
            DMA((NZ,)), DMA((NZ,)), DMA((4,)), DMA((4,)), DMA((4,)), DMA((4,)), DMA((3,)),
        ],
        compiler_params=pltpu.CompilerParams(collective_id=0, has_side_effects=True,
                                             vmem_limit_bytes=32 * 1024 * 1024),
        name="regroup_rows",
    )(slots, pos, pack)


def return_kernel(out, posz, back, posall, mid, s1, r1, ps, pr, s2, r2, loc):
    y, z, k, c = place()
    barrier = pltpu.get_barrier_semaphore()
    on_diag = y == c
    me = y * 2 + k

    def hello(d):
        pl.semaphore_signal(barrier, inc=1, device_id=d, device_id_type=MESH)

    @pl.loop(0, 8)
    def _(i):
        ys, ks = i // 2, lax.rem(i, 2)

        @pl.when(jnp.logical_not(on_diag & (i == me)))
        def _():
            hello(dev(ys, z, ks, y))

    @pl.loop(1, NZ)
    def _(i):
        hello(dev(y, lax.rem(z + i, NZ), k, c))

    @pl.when(on_diag)
    def _():
        pl.semaphore_wait(barrier, 22)

    @pl.when(jnp.logical_not(on_diag))
    def _():
        pl.semaphore_wait(barrier, 23)

    def stage1(i):
        kk, cc = lax.rem(i, 2), i // 2
        d = dev(c, z, kk, cc)
        a = pltpu.make_async_remote_copy(
            src_ref=out.at[kk, cc], dst_ref=mid.at[me], send_sem=s1.at[i], recv_sem=r1.at[me],
            device_id=d, device_id_type=MESH)
        b = pltpu.make_async_remote_copy(
            src_ref=posz, dst_ref=posall.at[me], send_sem=ps.at[i], recv_sem=pr.at[me],
            device_id=d, device_id_type=MESH)
        return a, b

    def is_me(i):
        return on_diag & (i == c * 2 + k)

    @pl.loop(0, 8)
    def _(i):
        @pl.when(is_me(i))
        def _():
            pltpu.make_async_copy(out.at[k, c], mid.at[me], r1.at[me]).start()
            pltpu.make_async_copy(posz, posall.at[me], pr.at[me]).start()

        @pl.when(jnp.logical_not(is_me(i)))
        def _():
            a, b = stage1(i)
            a.start()
            b.start()

    def arrived(i):
        return (pltpu.make_async_copy(mid.at[i], mid.at[i], r1.at[i]),
                pltpu.make_async_copy(posall.at[i], posall.at[i], pr.at[i]))

    @pl.loop(0, 8)
    def _(i):
        arrived(i)[0].wait()

    def stage2(i):
        zz = lax.rem(z + i, NZ)
        return pltpu.make_async_remote_copy(
            src_ref=mid.at[:, zz], dst_ref=back.at[z], send_sem=s2.at[i], recv_sem=r2.at[i],
            device_id=dev(y, zz, k, c), device_id_type=MESH)

    @pl.loop(1, NZ)
    def _(i):
        stage2(i).start()
    own = pltpu.make_async_copy(mid.at[:, z], back.at[z], loc.at[0])
    own.start()
    own.wait()

    @pl.loop(0, 8)
    def _(i):
        arrived(i)[1].wait()

        @pl.when(jnp.logical_not(is_me(i)))
        def _():
            a, b = stage1(i)
            a.wait_send()
            b.wait_send()

    @pl.loop(1, NZ)
    def _(i):
        stage2(i).wait()


def send_back(out, posz):
    DMA = pltpu.SemaphoreType.DMA
    vm = pl.BlockSpec(memory_space=pltpu.VMEM)
    return pl.pallas_call(
        return_kernel,
        out_shape=(
            jax.ShapeDtypeStruct((NZ, 8, 4, 128), jnp.bfloat16),
            jax.ShapeDtypeStruct((8, NZ, 1, 128), jnp.int32),
        ),
        in_specs=[vm, vm],
        out_specs=(vm, vm),
        scratch_shapes=[
            pltpu.VMEM((8, NZ, 4, 128), jnp.bfloat16),
            DMA((8,)), DMA((8,)), DMA((8,)), DMA((8,)), DMA((NZ,)), DMA((NZ,)), DMA((1,)),
        ],
        compiler_params=pltpu.CompilerParams(collective_id=1, has_side_effects=True,
                                             vmem_limit_bytes=32 * 1024 * 1024),
        name="return_rows",
    )(out, posz)
def iota(shape, dim):
    return lax.broadcasted_iota(jnp.int32, shape, dim)


def dot(a, b):
    return jnp.dot(a, b, preferred_element_type=jnp.float32)


def dot_nt(a, b):
    return lax.dot_general(a, b, (((1,), (1,)), ((), ())), preferred_element_type=jnp.float32)


def onehot(mask):
    return jnp.where(mask, 1.0, 0.0).astype(BF16)


def row_norm(values):
    center = values - jnp.mean(values, axis=-1, keepdims=True)
    spread = jnp.mean(center * center, axis=-1, keepdims=True)
    return (center * lax.rsqrt(spread + EPS)).astype(BF16)


def column_norm(values):
    center = values - jnp.mean(values, axis=0, keepdims=True)
    spread = jnp.mean(center * center, axis=0, keepdims=True)
    return (center * lax.rsqrt(spread + EPS)).astype(BF16)


def pool_kernel(raw, ids, hilbert, zpos, qkv, proj, fc1, fc2, slots, pos, pack):
    c = lax.axis_index("ch")
    target = hilbert[...]
    rel = jnp.where(target >= 0, (target >> 10) - c * 32, -1)
    hits = iota((32, 2048), 0) == rel
    hot = onehot(hits)
    upper = onehot(iota((256, 256), 0) < iota((256, 256), 1))
    before = jnp.zeros((32, 1), jnp.float32)
    index_rows = []
    for b in range(8):
        part = hot[:, b * 256:(b + 1) * 256]
        part32 = part.astype(jnp.float32)
        rank = dot(part, upper) + before
        rank = jnp.sum(rank * part32, axis=0, keepdims=True)
        before = before + jnp.sum(part32, axis=1, keepdims=True)
        r = rel[:, b * 256:(b + 1) * 256]
        slot = (r & 1) * 256 + (r >> 1) * 16 + rank.astype(jnp.int32)
        index_rows.append(jnp.where((r >= 0) & (r < 32), slot, -1))
    cell = jnp.zeros((512, 256), jnp.float32)
    for b in range(8):
        place_ = onehot(iota((512, 256), 0) == index_rows[b])
        low = iota((256, 256), 1) >= 128
        number = jnp.where(low, iota((256, 256), 0), b).astype(jnp.float32).astype(BF16)
        cell = cell + dot(place_, number)
    cell = cell[:, :128] * 256.0 + cell[:, 128:]
    total = jnp.zeros((512, 256), jnp.float32)
    one = jnp.ones((512, 128), BF16)
    points = ids[...].astype(jnp.float32)
    for b in range(6):
        member = jnp.concatenate(
            [onehot(cell == points[4 * b + j:4 * b + j + 1]) for j in range(4)], axis=1)
        rows = jnp.concatenate([raw[b * 512:(b + 1) * 512], one], axis=1)
        total = total + dot(member, rows)
    mean = (total[:, :128] / total[:, 128:]).astype(BF16)
    for kk in range(2):
        for zz in range(16):
            at = kk * 256 + zz * 16
            slots[kk, zz] = mean[at:at + 16]
    z_rows = zpos[...]
    z32 = z_rows.astype(jnp.float32)
    column = jnp.concatenate(
        [jnp.transpose(jnp.broadcast_to(z32[j:j + 1], (128, 128))) for j in range(8)], axis=0)
    split = jnp.zeros((32, 128), jnp.float32)
    for j in range(8):
        rank = jnp.sum(jnp.where(column < z32[j:j + 1], 1.0, 0.0), axis=0, keepdims=True)
        rank = rank.astype(jnp.int32)
        own = z_rows[j:j + 1] & 1023
        dest = rank >> 3
        z_of = (dest >> 1) & 15
        lane = ((dest >> 5) * 2 + (dest & 1)) * 8 + (rank & 7)
        sub = iota((32, 128), 0)
        digit = jnp.where(sub < 16, own >> 5, own & 31).astype(jnp.float32)
        left = jnp.where((sub & 15) == z_of, digit, 0.0).astype(BF16)
        right = onehot(iota((128, 128), 0) == lane)
        split = split + dot_nt(left, right)
    table = (split[:16] * 32.0 + split[16:]).astype(jnp.int32)
    for zz in range(16):
        pos[zz] = table[zz:zz + 1]
    eye = onehot(iota((256, 256), 0) == iota((256, 256), 1))
    eye64 = onehot(iota((64, 64), 0) == iota((64, 64), 1))
    for t in range(3):
        pack[t * 64:(t + 1) * 64] = dot_nt(eye64, qkv[t]).astype(BF16)
    pack[192:256] = dot_nt(eye64, proj[...]).astype(BF16)
    pack[256:512] = dot_nt(eye, fc1[...]).astype(BF16)
    pack[512:768] = dot_nt(eye, fc2[...]).astype(BF16)


def block_kernel(rows, counts, pool, wall, out, x_ref):
    c = lax.axis_index("ch")
    f32 = jnp.float32
    units = (counts[...] >> 7).astype(f32).astype(BF16)
    units = jnp.broadcast_to(units, (8, 128))
    source = iota((128, 2048), 1) >> 4
    held = dot(units, onehot(iota((128, 2048), 0) == source))[:1].astype(jnp.int32)
    first = dot(units, onehot(iota((128, 2048), 0) < source))[:1].astype(jnp.int32)
    within = iota((1, 2048), 1) & 15
    order = jnp.where(within < held, first + within, -1)
    x = jnp.zeros((1024, 128), f32)
    for b in range(8):
        sel = onehot(iota((1024, 256), 0) == order[:, b * 256:(b + 1) * 256])
        x = x + dot(sel, rows[b * 256:(b + 1) * 256])
    x = x.astype(BF16)
    x_ref[...] = x
    w = pool[...]
    normed = row_norm(dot(x, w).astype(BF16).astype(f32))
    wq = jnp.concatenate([wall[i, 0:64] for i in range(4)], axis=0)
    wk = jnp.concatenate([wall[i, 64:128] for i in range(4)], axis=0)
    wv = jnp.concatenate([wall[i, 128:192] for i in range(4)], axis=0)
    keys = dot_nt(normed, wk).astype(BF16)
    values = dot_nt(wv, normed).astype(BF16)
    t = iota((256, 256), 0)
    row = 8 * (((t >> 2) & 15) * 2 + ((t >> 6) & 1)) + 4 * (t >> 7) + (t & 3)
    mine = dot(onehot(iota((256, 256), 1) == row), x_ref[pl.ds(pl.multiple_of(c * 256, 256), 256)])
    features = dot(mine.astype(BF16), w).astype(BF16).astype(f32)
    query = dot_nt(wq, row_norm(features)).astype(BF16)
    head_of = iota((256, 256), 0) >> 4
    ones = jnp.ones((16, 1024), BF16)
    scale = 0.25 * 1.4426950408889634
    heads = []
    for h in range(16):
        only = jnp.where(head_of == h, query.astype(f32), 0.0).astype(BF16)
        scores = dot(keys, only)
        peak = jnp.max(scores, axis=0, keepdims=True)
        raised = jnp.exp2((scores - peak) * scale).astype(BF16)
        mix = dot(jnp.concatenate([values[h * 16:(h + 1) * 16], ones], axis=0), raised)
        heads.append((mix[:16] / mix[16:17]).astype(BF16))
    attended = jnp.concatenate(heads, axis=0)
    wp = jnp.concatenate([wall[i, 192:256] for i in range(4)], axis=0)
    middle = (jnp.transpose(features) + dot(wp, attended)).astype(BF16).astype(f32)
    normed2 = column_norm(middle)
    total = jnp.zeros((256, 256), f32)
    for i in range(4):
        v = dot(wall[i, 256:512], normed2)
        hidden = (v * (1.0 + lax.erf(v * 0.7071067811865476)) * 0.5).astype(BF16)
        total = total + dot(wall[i, 512:768], hidden)
    result = jnp.transpose(middle + total)
    for kk in range(2):
        for cc in range(4):
            both = [result[h * 128 + kk * 64:h * 128 + kk * 64 + 64, cc * 64:cc * 64 + 64] for h in range(2)]
            out[kk, cc] = jnp.concatenate(both, axis=1).reshape(16, 4, 128).astype(BF16)


def settle_kernel(back, posall, out):
    p = lax.axis_index("pts")
    me = (p // 32) * 2 + lax.rem(p, 2)
    f32 = jnp.float32
    got = back[...].astype(f32).reshape(512, 128).astype(BF16)
    table = posall[...].reshape(128, 128)
    pick = onehot(iota((8, 128), 1) == me * 8 + iota((8, 128), 0))
    digits = [dot_nt(pick, part.astype(f32).astype(BF16)).astype(BF16) for part in (table >> 5, table & 31)]
    k = iota((128, 512), 1)
    spread = onehot(iota((128, 512), 0) == ((k >> 2) & 7) * 16 + (k >> 5))
    full = dot(digits[0], spread) * 32.0 + dot(digits[1], spread)
    sub, lane = iota((8, 512), 0), iota((8, 512), 1)
    halves = []
    for h in range(2):
        want = jnp.sum(jnp.where(sub == h * 4 + (lane & 3), full, 0.0), axis=0, keepdims=True)
        want = want.astype(jnp.int32)
        halves.append(dot(onehot(iota((1024, 512), 0) == want), got))
    out[...] = (halves[0][:, :64] + halves[1][:, 64:]).astype(BF16)


def local(body, out_shape, scratch=(), name=None):
    n_out = len(out_shape) if isinstance(out_shape, tuple) else 1
    vm = pl.BlockSpec(memory_space=pltpu.VMEM)
    return pl.pallas_call(
        body, out_shape=out_shape,
        out_specs=(vm,) * n_out if isinstance(out_shape, tuple) else vm,
        scratch_shapes=scratch,
        compiler_params=pltpu.CompilerParams(vmem_limit_bytes=48 * 1024 * 1024), name=name)


def shards(raw_points, cell_ids, row_counts, hilbert_position, z_position,
           pool_weight, qkv_weight, proj_weight, fc1_weight, fc2_weight):
    S = jax.ShapeDtypeStruct
    slots, pos, pack = local(
        pool_kernel,
        (S((2, NZ, 16, 128), BF16), S((NZ, 1, 128), jnp.int32), S((768, 256), BF16)),
        name="pool_cells",
    )(raw_points, cell_ids.reshape(24, 128), hilbert_position, z_position.reshape(8, 128),
      qkv_weight, proj_weight, fc1_weight, fc2_weight)
    rows, posz, wall = regroup(slots, pos, pack)
    out = local(
        block_kernel, S((2, 4, NZ, 4, 128), BF16), scratch=[pltpu.VMEM((1024, 128), BF16)],
        name="block",
    )(rows.reshape(2048, 128), row_counts.reshape(1, 128), pool_weight, wall)
    back, posall = send_back(out, posz)
    return local(settle_kernel, S((1024, 64), BF16), name="settle")(back, posall)


def solution(mesh):
    in_specs = (P("pts", None), P("pts"), P(), P("pts", None), P("pts"), P(),
                P(None, None, "ch"), P(None, "ch"), P(None, "ch"), P("ch", None))
    return jax.shard_map(shards, mesh=mesh, in_specs=in_specs, out_specs=P("pts", "ch"),
                         check_vma=False)
```

time: 350 us -> 96.3 us (0.28); the launches traced: 343 us -> 94.9 us
  local copies, waits for them, and re-layouts: 132 us -> 7.78 us
  Pallas kernels: 0 us -> 87.1 us
  other arithmetic: 57.1 us -> 0 us
  starting transfers between devices: 52.4 us -> 0 us
  waiting for transfers between devices: 49.4 us -> 0 us
  blocking collectives: 26.6 us -> 0 us
  between operations: 14.2 us -> 0.07 us
  matrix products: 11 us -> 0 us
    pallas_call x0 -> x5, Pallas kernels: none -> 87.1 us  [the longest x1 42 us: regroup(): pl.pallas_call(gather_kernel, out_shape=(jax.ShapeDtypeStruct((4, NZ, 2,...]
    gather x29 -> x0, local copies, waits for them, and re-layouts: 82.8 us -> none  [the longest x23 30.2 us: slot_table(): jnp.searchsorted(ranked, jnp.arange(peer_count + 1, dtype=jnp.int32))]
    all_to_all x4 -> x0, starting transfers between devices: 52.4 us -> none  [the longest x1 20 us: shards(): lax.all_to_all(slot_rows, 'pts', split_axis=0, concat_axis=0, tiled=True)]
    all_to_all x4 -> x0, waiting for transfers between devices: 49.3 us -> none  [the longest x1 24.1 us: shards(): lax.all_to_all(outgoing, 'pts', split_axis=0, concat_axis=0, tiled=True)]
    scatter x6 -> x0, local copies, waits for them, and re-layouts: 43.4 us -> none  [the longest x4 30.7 us: fill_slots(): return padded.at[slot_index].set(values[ranking])[:total]]
    scatter-add x2 -> x0, other arithmetic: 40.9 us -> none  [the longest x1 22.3 us: shards(): jax.ops.segment_sum(jnp.ones(cell_ids.shape, jnp.float32), cell_ids, num_...]
    all_gather x2 -> x0, blocking collectives: 26.6 us -> none  [the longest x1 13.5 us: shards(): lax.all_gather(attended, 'ch', axis=1, tiled=True)]
    dot_general x11 -> x0, matrix products: 10.7 us -> none  [the longest x1 3.58 us: shards(): jnp.dot(hidden, fc2_weight, preferred_element_type=jnp.float32)]
  transfers between devices with their start and end apart: 5 -> 0, of which waited for: 3 -> 0; matrix products, arithmetic and copies ran while one was open for 29% -> 0% of each run, Pallas kernels for 0% -> 0%
where the time goes in v1:
time: 96.3 us; the launch traced here: 94.9 us
  Pallas kernels  87.1 us (90%)
  local copies, waits for them, and re-layouts  7.78 us (8%)
    pallas_call x1, Pallas kernels, regroup(): pl.pallas_call(gather_kernel, out_shape=(jax.ShapeDtypeStruct((4, NZ, 2,...  42 us
    pallas_call x1, Pallas kernels, send_back(): pl.pallas_call(return_kernel, out_shape=(jax.ShapeDtypeStruct((NZ, 8, 4,...  24.7 us
    pallas_call x1, Pallas kernels, shards(): local(block_kernel, S((2, 4, NZ, 4, 128), BF16), scratch=[pltpu.VMEM((102...  15.9 us
    unnamed x18, local copies, waits for them, and re-layouts  7 us
    pallas_call x1, Pallas kernels, shards(): local(pool_kernel, (S((2, NZ, 16, 128), BF16), S((NZ, 1, 128), jnp.int32)...  3.19 us

profile of v1, /device:TPU:6, one launch (start us, length us, event | category | flops | bytes accessed | tf_op | source)
XLA Modules:
  0.0 94.9 jit_solution(41537458708907917)
XLA Ops:
  0.0 0.0 copy-start.3
  0.0 0.0 copy-start.7
  0.0 0.9 copy.12.proj
  0.9 1.1 %copy.11.qkv = bf16[3,256,64]{2,1,0:T(8,128)(2,1)S(1)} copy(bf16[3,256,64]{1,2,0:T(8,128)(2,1)} %param.16) | data formatting | bytes 196608 | tf_op args[6]
  2.0 0.0 copy-start
  2.0 1.1 %copy-done = bf16[3072,128]{1,0:T(8,128)(2,1)S(1)} copy-done((bf16[3072,128]{1,0:T(8,128)(2,1)S(1)}, bf16[3072,128]{1,0:T(8,128)(2,1)}, u32[]{:S(2)}) %copy-start) | copy-done | bytes 786456
  3.1 0.0 copy-start.1
  3.1 0.9 copy-done.1
  4.0 0.0 copy-start.2
  4.0 0.9 copy-done.2
  4.9 0.0 copy-start.4
  4.9 0.7 copy-done.4
  5.6 0.0 copy-start.5
  5.6 0.7 copy-done.5
  6.3 0.0 copy-start.6
  6.3 0.7 copy-done.6
  7.0 3.2 %pool_cells.1 = (bf16[2,16,16,128]{3,2,1,0:T(8,128)(2,1)S(1)}, s32[16,1,128]{2,1,0:T(1,128)S(1)}, bf16[768,256]{1,0:T(8,128)(2,1)S(1)}) custom-call(bf16[3072,128]{1,0:T(8,128)(2,1)S(1)} %copy-done, s32[24,128]{1,0:T(8,128)S(1)} %bitcast.5, s32[1,2048]{1,0:T(1,128)S(1)} %copy-done.5, s32[8,128]{1,0:T(8,128)S(1)} %bitcast.6, ...), custom_call_target="tpu_custom_call" | custom-call | tf_op jit(solution)/shard_map/pool_cells/pallas_call | solution.py:479
  10.2 42.0 %regroup_rows.1 = (bf16[4,16,2,16,128]{4,3,2,1,0:T(8,128)(2,1)S(1)}, s32[16,1,128]{2,1,0:T(1,128)S(1)}, bf16[4,768,256]{2,1,0:T(8,128)(2,1)S(1)}) custom-call(bf16[2,16,16,128]{3,2,1,0:T(8,128)(2,1)S(1)} %get-tuple-element.13.slots, s32[16,1,128]{2,1,0:T(1,128)S(1)} %get-tuple-element.14.pos, bf16[768,256]{1,0:T(8,128)(2,1)S(1)} %get-tuple-element.15.pack), custom_call_target="tpu_custom_call" | custom-call | tf_op jit(solution)/shard_map/regroup_rows/pallas_call | solution.py:165
  52.3 0.0 copy-done.3
  52.3 0.0 copy-done.7
  52.3 15.9 %block.1.out = bf16[2,4,16,4,128]{4,3,2,1,0:T(4,128)(2,1)S(1)} custom-call(bf16[2048,128]{1,0:T(8,128)(2,1)S(1)} %bitcast.4, s32[1,128]{1,0:T(1,128)S(1)} %bitcast.7, bf16[128,256]{1,0:T(8,128)(2,1)S(1)} %copy-done.3, bf16[4,768,256]{2,1,0:T(8,128)(2,1)S(1)} %get-tuple-element.17.wall), custom_call_target="tpu_custom_call" | custom-call | tf_op jit(solution)/shard_map/block/pallas_call | solution.py:486
  68.2 24.7 %return_rows.1 = (bf16[16,8,4,128]{3,2,1,0:T(4,128)(2,1)S(1)}, s32[8,16,1,128]{3,2,1,0:T(1,128)S(1)}) custom-call(bf16[2,4,16,4,128]{4,3,2,1,0:T(4,128)(2,1)S(1)} %block.1.out, s32[16,1,128]{2,1,0:T(1,128)S(1)} %get-tuple-element.18.posz), custom_call_target="tpu_custom_call" | custom-call | tf_op jit(solution)/shard_map/return_rows/pallas_call | solution.py:280
  93.0 1.2 %settle.1 = bf16[1024,64]{1,0:T(8,128)(2,1)S(1)} custom-call(bf16[16,8,4,128]{3,2,1,0:T(4,128)(2,1)S(1)} %get-tuple-element.19.back, s32[8,16,1,128]{3,2,1,0:T(1,128)S(1)} %get-tuple-element.20.posall), custom_call_target="tpu_custom_call" | custom-call | tf_op jit(solution)/shard_map/settle/pallas_call | solution.py:491
  94.1 0.8 copy.13
Async XLA Ops:
  0.0 52.3 %copy-start.3 = (bf16[128,256]{1,0:T(8,128)(2,1)S(1)}, bf16[128,256]{1,0:T(8,128)(2,1)}, u32[]{:S(2)}) copy-start(bf16[128,256]{1,0:T(8,128)(2,1)} %pool.1) | copy-start | bytes 196612
  0.0 52.3 %copy-start.7 = (s32[128]{0:T(128)S(1)}, s32[128]{0:T(128)}, u32[]{:S(2)}) copy-start(s32[128]{0:T(128)} %param.12) | copy-start | bytes 1540
  2.0 1.1 %copy-start = (bf16[3072,128]{1,0:T(8,128)(2,1)S(1)}, bf16[3072,128]{1,0:T(8,128)(2,1)}, u32[]{:S(2)}) copy-start(bf16[3072,128]{1,0:T(8,128)(2,1)} %raw.1) | copy-start | bytes 2359300
  3.1 0.9 copy-start.1
  4.0 0.9 copy-start.2
  4.9 0.7 copy-start.4
  5.6 0.7 copy-start.5
  6.3 0.7 copy-start.6

commit v2 on v0

v2 whole, which is shorter than its diff:
```python
import jax
import jax.numpy as jnp
from jax import lax
from jax.experimental import pallas as pl
from jax.experimental.pallas import tpu as pltpu
from jax.sharding import PartitionSpec as P

BF16 = jnp.bfloat16
EPS = 1e-5


def iota(shape, dim):
    return lax.broadcasted_iota(jnp.int32, shape, dim)


def dot(a, b):
    return jnp.dot(a, b, preferred_element_type=jnp.float32)


def dot_nt(a, b):
    return lax.dot_general(a, b, (((1,), (1,)), ((), ())), preferred_element_type=jnp.float32)


def onehot(mask):
    return jnp.where(mask, 1.0, 0.0).astype(BF16)


def row_norm(values):
    center = values - jnp.mean(values, axis=-1, keepdims=True)
    spread = jnp.mean(center * center, axis=-1, keepdims=True)
    return (center * lax.rsqrt(spread + EPS)).astype(BF16)


MESH = pl.DeviceIdType.MESH
NZ = 16
LIMIT = 64 * 1024 * 1024 - 65536
ANY = pl.BlockSpec(memory_space=pltpu.HBM)
VM = pl.BlockSpec(memory_space=pltpu.VMEM)


def place():
    p, c = lax.axis_index("pts"), lax.axis_index("ch")
    return p // 32, lax.rem(p // 2, NZ), lax.rem(p, 2), c


def dev(y, z, k, c):
    return (y * 32 + z * 2 + k, c)


def hop(j):
    return lax.rem(j, 2) * ((j + 1) // 2) + (1 - lax.rem(j, 2)) * (NZ - j // 2)


def layer_kernel(raw_h, ids_h, hilbert_h, zpos_h, counts_h, pool_h, qkv_h, proj_h, fc1_h, fc2_h,
                 result_t,
                 raw, ids, hilbert, zpos, counts, pool, wq, wp, w1, w2,
                 slots, pos, posz, posall, mid, rows, acc, out, mid2,
                 lsem, ps, pr, s2, r2, s3, r3, ws, wr, fs, fr, qs, qr, c1s, c1r, c2s, c2r, back, placing):
    y, z, k, c = place()
    me = y * 2 + k
    f32 = jnp.float32
    on_diag = y == c
    barrier = pltpu.get_barrier_semaphore()

    def hello(d):
        pl.semaphore_signal(barrier, inc=1, device_id=d, device_id_type=MESH)

    hello(dev(y, z, 1 - k, c))
    for i in range(1, 4):
        hello(dev(y, z, k, lax.rem(c + i, 4)))

    @pl.loop(1, NZ)
    def _(i):
        hello(dev(y, lax.rem(z + i, NZ), k, c))

    @pl.loop(0, 8)
    def _(i):
        @pl.when(jnp.logical_not(on_diag & (i == me)))
        def _():
            hello(dev(i // 2, z, lax.rem(i, 2), y))

    loads = [pltpu.make_async_copy(a, b, lsem.at[i]) for i, (a, b) in enumerate((
        (hilbert_h, hilbert), (zpos_h, zpos), (ids_h, ids), (raw_h, raw), (counts_h, counts), (pool_h, pool),
        (qkv_h, wq.at[c]), (proj_h, wp.at[c]), (fc1_h, w1.at[c]), (fc2_h, w2.at[c])))]
    for load in loads:
        load.start()

    loads[0].wait()
    target = hilbert[...]
    rel = jnp.where(target >= 0, (target >> 10) - c * 32, -1)
    hot = onehot(iota((32, 2048), 0) == rel)
    upper = onehot(iota((256, 256), 0) < iota((256, 256), 1))
    before = jnp.zeros((32, 1), f32)
    cell = jnp.zeros((512, 256), f32)
    for b in range(8):
        part = hot[:, b * 256:(b + 1) * 256]
        part32 = part.astype(f32)
        rank = jnp.sum((dot(part, upper) + before) * part32, axis=0, keepdims=True)
        before = before + jnp.sum(part32, axis=1, keepdims=True)
        r = rel[:, b * 256:(b + 1) * 256]
        index = jnp.where((r >= 0) & (r < 32), r * 16 + rank.astype(jnp.int32), -1)
        number = jnp.where(iota((256, 256), 1) >= 128, iota((256, 256), 0), b)
        cell = cell + dot(onehot(iota((512, 256), 0) == index), number.astype(f32).astype(BF16))
    cell = cell[:, :128] * 256.0 + cell[:, 128:]

    @pl.when(on_diag)
    def _():
        pl.semaphore_wait(barrier, 26)

    @pl.when(jnp.logical_not(on_diag))
    def _():
        pl.semaphore_wait(barrier, 27)

    def parts(a):
        return ((qkv_h, wq, 32, True), (fc1_h, w1, 128, False), (proj_h, wp, 32, False),
                (fc2_h, w2, 128, False))[a]

    def weight_x(a, i):
        src, dst, size, deep = parts(a)
        half = pl.ds(pl.multiple_of(k * size, size), size)
        return pltpu.make_async_remote_copy(
            src_ref=src.at[:, half] if deep else src.at[half],
            dst_ref=dst.at[c, :, half] if deep else dst.at[c, half],
            send_sem=ws.at[a, i], recv_sem=wr.at[a, i],
            device_id=dev(y, z, k, lax.rem(c + i, 4)), device_id_type=MESH)

    def weight_core(a, i):
        _, dst, size, deep = parts(a)
        half = pl.ds(pl.multiple_of(k * size, size), size)
        owner = lax.rem(c - i + 4, 4)
        at = dst.at[owner, :, half] if deep else dst.at[owner, half]
        return pltpu.make_async_remote_copy(
            src_ref=at, dst_ref=at, send_sem=fs.at[a, i], recv_sem=fr.at[a, i],
            device_id=dev(y, z, 1 - k, c), device_id_type=MESH)

    for a in range(4):
        for i in range(1, 4):
            weight_x(a, i).start()

    loads[2].wait()
    loads[3].wait()
    total = jnp.zeros((512, 256), f32)
    one = jnp.ones((512, 128), BF16)
    points = ids[...].astype(f32)
    for b in range(6):
        member = jnp.concatenate(
            [onehot(cell == points[4 * b + j:4 * b + j + 1]) for j in range(4)], axis=1)
        total = total + dot(member, jnp.concatenate([raw[b * 512:(b + 1) * 512], one], axis=1))
    mean = (total[:, :128] / total[:, 128:]).astype(BF16)
    for zz in range(NZ):
        for kk in range(2):
            slots[zz, kk] = mean[zz * 32 + kk * 16:zz * 32 + kk * 16 + 16]

    def rows_z(j):
        zz = lax.rem(z + hop(j), NZ)
        return pltpu.make_async_remote_copy(
            src_ref=slots.at[zz], dst_ref=mid.at[j], send_sem=s2.at[j], recv_sem=r2.at[j],
            device_id=dev(y, zz, k, c), device_id_type=MESH)

    @pl.loop(1, NZ)
    def _(j):
        rows_z(j).start()
    own_z = pltpu.make_async_copy(slots.at[z], mid.at[0], r2.at[0])
    own_z.start()

    def is_me(i):
        return on_diag & (i == c * 2 + k)

    def on(g, i):
        kk, cc = lax.rem(i, 2), i // 2
        return pltpu.make_async_remote_copy(
            src_ref=mid.at[2 * g:2 * g + 2, kk], dst_ref=rows.at[2 * g:2 * g + 2, me],
            send_sem=s3.at[g, i], recv_sem=r3.at[g, me],
            device_id=dev(c, z, kk, cc), device_id_type=MESH)

    def on_start(g):
        @pl.loop(0, 8)
        def _(i):
            @pl.when(is_me(i))
            def _():
                pltpu.make_async_copy(mid.at[2 * g:2 * g + 2, k], rows.at[2 * g:2 * g + 2, me],
                                      r3.at[g, me]).start()

            @pl.when(jnp.logical_not(is_me(i)))
            def _():
                on(g, i).start()

    def on_arrived(g):
        @pl.loop(0, 8)
        def _(i):
            block = rows.at[2 * g:2 * g + 2, i]
            pltpu.make_async_copy(block, block, r3.at[g, i]).wait()

    loads[1].wait()
    z_rows = zpos[...]
    z32 = z_rows.astype(f32)
    column = jnp.concatenate(
        [jnp.transpose(jnp.broadcast_to(z32[j:j + 1], (128, 128))) for j in range(8)], axis=0)
    split = jnp.zeros((32, 128), f32)
    for j in range(8):
        rank = jnp.sum(jnp.where(column < z32[j:j + 1], 1.0, 0.0), axis=0, keepdims=True)
        rank = rank.astype(jnp.int32)
        own = z_rows[j:j + 1] & 1023
        dest = rank >> 3
        lane = ((dest >> 5) * 2 + (dest & 1)) * 8 + (rank & 7)
        sub = iota((32, 128), 0)
        digit = jnp.where(sub < 16, own >> 5, own & 31).astype(f32)
        left = jnp.where((sub & 15) == ((dest >> 1) & 15), digit, 0.0).astype(BF16)
        split = split + dot_nt(left, onehot(iota((128, 128), 0) == lane))
    table = (split[:16] * 32.0 + split[16:]).astype(jnp.int32)
    for zz in range(NZ):
        pos[zz] = table[zz:zz + 1]

    def pos_z(j):
        zz = lax.rem(z + j, NZ)
        return pltpu.make_async_remote_copy(
            src_ref=pos.at[zz], dst_ref=posz.at[z], send_sem=ps.at[j], recv_sem=pr.at[j],
            device_id=dev(y, zz, k, c), device_id_type=MESH)

    def pos_arrived(j):
        zs = lax.rem(z - j + NZ, NZ)
        return pltpu.make_async_copy(posz.at[zs], posz.at[zs], pr.at[j])

    own_pos = pltpu.make_async_copy(pos.at[z], posz.at[z], pr.at[0])
    own_pos.start()

    loads[4].wait()
    units = jnp.broadcast_to((counts[...] >> 7).astype(f32).astype(BF16), (8, 128))
    col = iota((128, 2048), 1)
    hop_no, from_yc = col >> 7, (col >> 4) & 7
    away = jnp.where((hop_no & 1) == 1, (hop_no + 1) >> 1, NZ - (hop_no >> 1))
    source = (from_yc >> 1) * 32 + ((z + NZ - away) & 15) * 2 + (from_yc & 1)
    held = dot(units, onehot(iota((128, 2048), 0) == source))[:1].astype(jnp.int32)
    first = dot(units, onehot(iota((128, 2048), 0) < source))[:1].astype(jnp.int32)
    within = iota((1, 2048), 1) & 15
    order = jnp.where(within < held, first + within, -1)

    def gather_group(g):
        on_arrived(g)
        sel = onehot(iota((1024, 256), 0) == order[:, g * 256:(g + 1) * 256])
        piece = dot(sel, rows[2 * g:2 * g + 2].reshape(256, 128))
        if g == 0:
            acc[...] = piece
        else:
            acc[...] += piece

    LAG = 3
    for g in range(8):
        for j in (2 * g, 2 * g + 1):
            pltpu.make_async_copy(mid.at[j], mid.at[j], r2.at[j]).wait()
        on_start(g)
        if g == 0:
            @pl.loop(1, NZ)
            def _(j):
                pos_z(j).start()
        if g >= LAG:
            gather_group(g - LAG)
    for a in range(4):
        for i in range(1, 4):
            weight_x(a, i).wait_recv()
            weight_core(a, i).start()
        if a == 0:
            for g in range(8 - LAG, 8):
                gather_group(g)

    @pl.loop(0, NZ)
    def _(j):
        pos_arrived(j).wait()

    def pos_on(i):
        return pltpu.make_async_remote_copy(
            src_ref=posz, dst_ref=posall.at[me], send_sem=qs.at[i], recv_sem=qr.at[me],
            device_id=dev(c, z, lax.rem(i, 2), i // 2), device_id_type=MESH)

    @pl.loop(0, 8)
    def _(i):
        @pl.when(is_me(i))
        def _():
            pltpu.make_async_copy(posz, posall.at[me], qr.at[me]).start()

        @pl.when(jnp.logical_not(is_me(i)))
        def _():
            pos_on(i).start()

    x = acc[...].astype(BF16)
    loads[5].wait()
    w = pool[...]
    normed = row_norm(dot(x, w).astype(BF16).astype(f32))
    t = iota((256, 256), 0)
    row = 8 * (((t >> 2) & 15) * 2 + ((t >> 6) & 1)) + 4 * (t >> 7) + (t & 3)
    quarter = acc[pl.ds(pl.multiple_of(c * 256, 256), 256)].astype(BF16)
    mine = dot(onehot(iota((256, 256), 1) == row), quarter)
    features = dot(mine.astype(BF16), w).astype(BF16).astype(f32)
    loads[6].wait()
    for i in range(1, 4):
        weight_core(0, i).wait_recv()
    keys = dot_nt(normed, wq[:, 1].reshape(256, 256)).astype(BF16)
    values = dot_nt(wq[:, 2].reshape(256, 256), normed).astype(BF16)
    query = dot_nt(wq[:, 0].reshape(256, 256), row_norm(features)).astype(BF16)
    head_of = iota((256, 256), 0) >> 4
    ones = jnp.ones((16, 1024), BF16)
    scale = 0.25 * 1.4426950408889634
    heads = []
    for h in range(16):
        only = jnp.where(head_of == h, query.astype(f32), 0.0).astype(BF16)
        scores = dot(keys, only)
        peak = jnp.max(scores, axis=0, keepdims=True)
        raised = jnp.exp2((scores - peak) * scale).astype(BF16)
        mix = dot(jnp.concatenate([values[h * 16:(h + 1) * 16], ones], axis=0), raised)
        heads.append((mix[:16] / mix[16:17]).astype(BF16))
    attended = jnp.concatenate(heads, axis=0)
    for load in loads[7:]:
        load.wait()
    for a in range(1, 4):
        for i in range(1, 4):
            weight_core(a, i).wait_recv()
    mixture = jnp.transpose(dot(wp[...].reshape(256, 256), attended))
    middle = (features + mixture).astype(BF16).astype(f32)
    normed2 = row_norm(middle)
    result = middle
    for i in range(4):
        v = dot(normed2, w1[i])
        hidden = (v * (1.0 + lax.erf(v * 0.7071067811865476)) * 0.5).astype(BF16)
        result = result + dot(hidden, w2[i])
    for kk in range(2):
        for cc in range(4):
            both = [result[h * 128 + kk * 64:h * 128 + kk * 64 + 64, cc * 64:cc * 64 + 64] for h in range(2)]
            out[kk, cc] = jnp.concatenate(both, axis=1).reshape(NZ, 4, 128).astype(BF16)

    def back_xy(i):
        kk, cc = lax.rem(i, 2), i // 2
        return pltpu.make_async_remote_copy(
            src_ref=out.at[kk, cc], dst_ref=mid2.at[me], send_sem=c1s.at[i], recv_sem=c1r.at[me],
            device_id=dev(c, z, kk, cc), device_id_type=MESH)

    @pl.loop(0, 8)
    def _(i):
        @pl.when(is_me(i))
        def _():
            pltpu.make_async_copy(out.at[k, c], mid2.at[me], c1r.at[me]).start()

        @pl.when(jnp.logical_not(is_me(i)))
        def _():
            back_xy(i).start()

    @pl.loop(0, 8)
    def _(i):
        pltpu.make_async_copy(posall.at[i], posall.at[i], qr.at[i]).wait()
    table = posall[...].reshape(128, 128)
    pick = onehot(iota((8, 128), 1) == me * 8 + iota((8, 128), 0))
    digits = [dot_nt(pick, part.astype(f32).astype(BF16)).astype(BF16) for part in (table >> 5, table & 31)]
    n = iota((128, 512), 1)
    spread = onehot(iota((128, 512), 0) == ((n >> 2) & 7) * 16 + (n >> 5))
    full = dot(digits[0], spread) * 32.0 + dot(digits[1], spread)
    sub, lane = iota((8, 512), 0), iota((8, 512), 1)
    wants = []
    for h in range(2):
        want = jnp.sum(jnp.where(sub == h * 4 + (lane & 3), full, 0.0), axis=0, keepdims=True)
        wants.append(want.astype(jnp.int32))

    @pl.loop(0, 8)
    def _(i):
        pltpu.make_async_copy(mid2.at[i], mid2.at[i], c1r.at[i]).wait()

    def back_z(i):
        zz = lax.rem(z + i, NZ)
        return pltpu.make_async_remote_copy(
            src_ref=mid2.at[:, zz], dst_ref=back.at[z], send_sem=c2s.at[i], recv_sem=c2r.at[i],
            device_id=dev(y, zz, k, c), device_id_type=MESH)

    @pl.loop(1, NZ)
    def _(i):
        back_z(i).start()
    own_back = pltpu.make_async_copy(mid2.at[:, z], back.at[z], c2r.at[0])
    own_back.start()
    for h in range(2):
        placing[h] = onehot(iota((1024, 512), 0) == wants[h])

    for a in range(4):
        for i in range(1, 4):
            weight_x(a, i).wait_send()
            weight_core(a, i).wait_send()

    @pl.loop(1, NZ)
    def _(j):
        rows_z(j).wait_send()
        pos_z(j).wait_send()

    @pl.loop(0, 8)
    def _(i):
        @pl.when(jnp.logical_not(is_me(i)))
        def _():
            pos_on(i).wait_send()
            back_xy(i).wait_send()
            for g in range(8):
                on(g, i).wait_send()
    own_back.wait()

    @pl.loop(1, NZ)
    def _(i):
        back_z(i).wait()
    got = jnp.transpose(back[...].astype(f32).reshape(512, 128)).astype(BF16)
    result_t[...] = (dot_nt(got[:64], placing[0]) + dot_nt(got[64:], placing[1])).astype(BF16)


def shards(raw_points, cell_ids, row_counts, hilbert_position, z_position,
           pool_weight, qkv_weight, proj_weight, fc1_weight, fc2_weight):
    S, V, I32 = jax.ShapeDtypeStruct, pltpu.VMEM, jnp.int32

    def sems(*shape):
        return pltpu.SemaphoreType.DMA(shape)
    out = pl.pallas_call(
        layer_kernel,
        out_shape=S((64, 1024), BF16),
        in_specs=[ANY] * 10,
        out_specs=VM,
        scratch_shapes=[
            V((3072, 128), BF16), V((24, 128), I32), V((1, 2048), I32), V((8, 128), I32), V((1, 128), I32),
            V((128, 256), BF16), V((4, 3, 64, 256), BF16), V((4, 64, 256), BF16), V((4, 256, 256), BF16),
            V((4, 256, 256), BF16),
            V((NZ, 2, 16, 128), BF16), V((NZ, 1, 128), I32), V((NZ, 1, 128), I32), V((8, NZ, 1, 128), I32),
            V((NZ, 2, 16, 128), BF16), V((NZ, 8, 16, 128), BF16), V((1024, 128), jnp.float32),
            V((2, 4, NZ, 4, 128), BF16), V((8, NZ, 4, 128), BF16),
            sems(10), sems(NZ), sems(NZ), sems(NZ), sems(NZ), sems(8, 8), sems(8, 8),
            sems(4, 4), sems(4, 4), sems(4, 4), sems(4, 4), sems(8), sems(8), sems(8), sems(8), sems(NZ), sems(NZ),
            V((NZ, 8, 4, 128), BF16), V((2, 1024, 512), BF16),
        ],
        compiler_params=pltpu.CompilerParams(collective_id=0, has_side_effects=True,
                                             vmem_limit_bytes=LIMIT),
        name="layer",
    )(raw_points, cell_ids.reshape(24, 128), hilbert_position, z_position.reshape(8, 128),
      row_counts.reshape(1, 128), pool_weight, jnp.transpose(qkv_weight, (0, 2, 1)), proj_weight.T,
      fc1_weight, fc2_weight)
    return out.T


def solution(mesh):
    in_specs = (P("pts", None), P("pts"), P(), P("pts", None), P("pts"), P(),
                P(None, None, "ch"), P(None, "ch"), P(None, "ch"), P("ch", None))
    return jax.shard_map(shards, mesh=mesh, in_specs=in_specs, out_specs=P("pts", "ch"),
                         check_vma=False)
```

time: 350 us -> 70.5 us (0.20); the launches traced: 343 us -> 70 us
  local copies, waits for them, and re-layouts: 132 us -> 1.57 us
  Pallas kernels: 0 us -> 68.5 us
  other arithmetic: 57.1 us -> 0 us
  starting transfers between devices: 52.4 us -> 0 us
  waiting for transfers between devices: 49.4 us -> 0 us
  blocking collectives: 26.6 us -> 0 us
  between operations: 14.2 us -> 0.01 us
  matrix products: 11 us -> 0 us
    gather x29 -> x0, local copies, waits for them, and re-layouts: 82.8 us -> none  [the longest x23 30.2 us: slot_table(): jnp.searchsorted(ranked, jnp.arange(peer_count + 1, dtype=jnp.int32))]
    pallas_call x0 -> x1, Pallas kernels: none -> 68.5 us  [shards(): pl.pallas_call(layer_kernel, out_shape=S((64, 1024), BF16), in_specs=[ANY...]
    all_to_all x4 -> x0, starting transfers between devices: 52.4 us -> none  [the longest x1 20 us: shards(): lax.all_to_all(slot_rows, 'pts', split_axis=0, concat_axis=0, tiled=True)]
    all_to_all x4 -> x0, waiting for transfers between devices: 49.3 us -> none  [the longest x1 24.1 us: shards(): lax.all_to_all(outgoing, 'pts', split_axis=0, concat_axis=0, tiled=True)]
    scatter x6 -> x0, local copies, waits for them, and re-layouts: 43.4 us -> none  [the longest x4 30.7 us: fill_slots(): return padded.at[slot_index].set(values[ranking])[:total]]
    scatter-add x2 -> x0, other arithmetic: 40.9 us -> none  [the longest x1 22.3 us: shards(): jax.ops.segment_sum(jnp.ones(cell_ids.shape, jnp.float32), cell_ids, num_...]
    all_gather x2 -> x0, blocking collectives: 26.6 us -> none  [the longest x1 13.5 us: shards(): lax.all_gather(attended, 'ch', axis=1, tiled=True)]
    dot_general x11 -> x0, matrix products: 10.7 us -> none  [the longest x1 3.58 us: shards(): jnp.dot(hidden, fc2_weight, preferred_element_type=jnp.float32)]
  transfers between devices with their start and end apart: 5 -> 0, of which waited for: 3 -> 0; matrix products, arithmetic and copies ran while one was open for 29% -> 0% of each run, Pallas kernels for 0% -> 0%
where the time goes in v2:
time: 70.5 us; the launch traced here: 70 us
  Pallas kernels  68.5 us (97%)
  local copies, waits for them, and re-layouts  1.57 us (2%)
    pallas_call x1, Pallas kernels, shards(): pl.pallas_call(layer_kernel, out_shape=S((64, 1024), BF16), in_specs=[ANY...  68.5 us
    unnamed x1, local copies, waits for them, and re-layouts  1.57 us

profile of v2, /device:TPU:6, one launch (start us, length us, event | category | flops | bytes accessed | tf_op | source)
XLA Modules:
  0.0 70.0 jit_solution(2604239340099588310)
XLA Ops:
  0.0 68.5 %layer.1 = bf16[64,1024]{1,0:T(8,128)(2,1)} custom-call(bf16[3072,128]{1,0:T(8,128)(2,1)} %raw_h.1, s32[24,128]{1,0:T(8,128)} %bitcast.9, s32[1,2048]{1,0:T(1,128)} %hilbert_h.1, s32[8,128]{1,0:T(8,128)} %bitcast.10, s32[1,128]{1,0:T(1,128)} %bitcast.11, bf16[128,256]{1,0:T(8,128)(2,1)} %pool_h.1, bf16[3,64,256]{2,1,0:T(8,128)(2,1)} %bitcast.7, ...), custom_call_target="tpu_custom_call" | custom-call | tf_op jit(solution)/shard_map/layer/pallas_call | solution.py:412
  68.5 1.6 %copy.12 = bf16[1024,64]{0,1:T(8,128)(2,1)} copy(bf16[1024,64]{0,1:T(8,128)(2,1)} %bitcast.6) | data formatting | bytes 262144

commit v3 on v2

--- a/solution.py
+++ b/solution.py
@@ -133,9 +133,8 @@
             src_ref=at, dst_ref=at, send_sem=fs.at[a, i], recv_sem=fr.at[a, i],
             device_id=dev(y, z, 1 - k, c), device_id_type=MESH)
 
-    for a in range(4):
-        for i in range(1, 4):
-            weight_x(a, i).start()
+    for i in range(1, 4):
+        weight_x(0, i).start()
 
     loads[2].wait()
     loads[3].wait()
@@ -159,7 +158,7 @@
 
     @pl.loop(1, NZ)
     def _(j):
-        rows_z(j).start()
+        rows_z(NZ - j).start()
     own_z = pltpu.make_async_copy(slots.at[z], mid.at[0], r2.at[0])
     own_z.start()
 
@@ -244,7 +243,6 @@
         else:
             acc[...] += piece
 
-    LAG = 3
     for g in range(8):
         for j in (2 * g, 2 * g + 1):
             pltpu.make_async_copy(mid.at[j], mid.at[j], r2.at[j]).wait()
@@ -253,15 +251,14 @@
             @pl.loop(1, NZ)
             def _(j):
                 pos_z(j).start()
-        if g >= LAG:
-            gather_group(g - LAG)
-    for a in range(4):
+    for a in range(1, 4):
         for i in range(1, 4):
-            weight_x(a, i).wait_recv()
-            weight_core(a, i).start()
-        if a == 0:
-            for g in range(8 - LAG, 8):
-                gather_group(g)
+            weight_x(a, i).start()
+    for i in range(1, 4):
+        weight_x(0, i).wait_recv()
+        weight_core(0, i).start()
+    for g in range(8):
+        gather_group(g)
 
     @pl.loop(0, NZ)
     def _(j):
@@ -287,61 +284,95 @@
     w = pool[...]
     normed = row_norm(dot(x, w).astype(BF16).astype(f32))
     t = iota((256, 256), 0)
-    row = 8 * (((t >> 2) & 15) * 2 + ((t >> 6) & 1)) + 4 * (t >> 7) + (t & 3)
+    hop_no = 15 - ((t >> 7) * 8 + ((t >> 2) & 7))
+    away = jnp.where((hop_no & 1) == 1, (hop_no + 1) >> 1, NZ - (hop_no >> 1))
+    row = 8 * (((z + away) & 15) * 2 + ((t >> 5) & 1)) + 4 * ((t >> 6) & 1) + (t & 3)
     quarter = acc[pl.ds(pl.multiple_of(c * 256, 256), 256)].astype(BF16)
     mine = dot(onehot(iota((256, 256), 1) == row), quarter)
     features = dot(mine.astype(BF16), w).astype(BF16).astype(f32)
     loads[6].wait()
     for i in range(1, 4):
         weight_core(0, i).wait_recv()
-    keys = dot_nt(normed, wq[:, 1].reshape(256, 256)).astype(BF16)
-    values = dot_nt(wq[:, 2].reshape(256, 256), normed).astype(BF16)
-    query = dot_nt(wq[:, 0].reshape(256, 256), row_norm(features)).astype(BF16)
-    head_of = iota((256, 256), 0) >> 4
-    ones = jnp.ones((16, 1024), BF16)
+    keys = dot_nt(wq[:, 1].reshape(256, 256), normed).astype(BF16)
+    values = dot_nt(normed, wq[:, 2].reshape(256, 256)).astype(BF16)
+    query = dot_nt(row_norm(features), wq[:, 0].reshape(256, 256)).astype(BF16).astype(f32)
+    head_of = iota((256, 256), 1) >> 4
+    ones = jnp.ones((1024, 128), BF16)
+    summed = [jnp.concatenate([values[:, u * 128:(u + 1) * 128], ones], axis=1) for u in range(2)]
     scale = 0.25 * 1.4426950408889634
-    heads = []
+
+    def score(h):
+        return dot(jnp.where(head_of == h, query, 0.0).astype(BF16), keys)
+
+    lane_head = iota((256, 128), 1) >> 4
+    sides = [jnp.zeros((256, 128), f32)] * 2
+    scores = score(0)
     for h in range(16):
-        only = jnp.where(head_of == h, query.astype(f32), 0.0).astype(BF16)
-        scores = dot(keys, only)
-        peak = jnp.max(scores, axis=0, keepdims=True)
-        raised = jnp.exp2((scores - peak) * scale).astype(BF16)
-        mix = dot(jnp.concatenate([values[h * 16:(h + 1) * 16], ones], axis=0), raised)
-        heads.append((mix[:16] / mix[16:17]).astype(BF16))
-    attended = jnp.concatenate(heads, axis=0)
+        later = score(h + 1) if h < 15 else None
+        if h == 12:
+            for a in range(1, 4):
+                for i in range(1, 4):
+                    weight_x(a, i).wait_recv()
+                    weight_core(a, i).start()
+        peak = jnp.max(scores, axis=1, keepdims=True)
+        mix = dot(jnp.exp2((scores - peak) * scale).astype(BF16), summed[h // 8])
+        sides[h // 8] = jnp.where(lane_head == h % 8, mix[:, :128] / mix[:, 128:], sides[h // 8])
+        scores = later
+    attended = jnp.concatenate(sides, axis=1).astype(BF16)
     for load in loads[7:]:
         load.wait()
     for a in range(1, 4):
         for i in range(1, 4):
             weight_core(a, i).wait_recv()
-    mixture = jnp.transpose(dot(wp[...].reshape(256, 256), attended))
-    middle = (features + mixture).astype(BF16).astype(f32)
-    normed2 = row_norm(middle)
-    result = middle
-    for i in range(4):
-        v = dot(normed2, w1[i])
-        hidden = (v * (1.0 + lax.erf(v * 0.7071067811865476)) * 0.5).astype(BF16)
-        result = result + dot(hidden, w2[i])
-    for kk in range(2):
-        for cc in range(4):
-            both = [result[h * 128 + kk * 64:h * 128 + kk * 64 + 64, cc * 64:cc * 64 + 64] for h in range(2)]
-            out[kk, cc] = jnp.concatenate(both, axis=1).reshape(NZ, 4, 128).astype(BF16)
-
-    def back_xy(i):
+    middle = (features + dot_nt(attended, wp[...].reshape(256, 256))).astype(BF16).astype(f32)
+
+    def back_xy(q, i):
         kk, cc = lax.rem(i, 2), i // 2
         return pltpu.make_async_remote_copy(
-            src_ref=out.at[kk, cc], dst_ref=mid2.at[me], send_sem=c1s.at[i], recv_sem=c1r.at[me],
+            src_ref=out.at[q, kk, cc], dst_ref=mid2.at[q, me], send_sem=c1s.at[q, i], recv_sem=c1r.at[q, me],
             device_id=dev(c, z, kk, cc), device_id_type=MESH)
 
+    def forward(q):
+        part = middle[q * 128:(q + 1) * 128]
+        normed2 = row_norm(part)
+        for i in range(4):
+            v = dot(normed2, w1[i])
+            hidden = (v * (1.0 + lax.erf(v * 0.7071067811865476)) * 0.5).astype(BF16)
+            part = part + dot(hidden, w2[i])
+        for kk in range(2):
+            for cc in range(4):
+                both = [part[h * 64 + kk * 32:h * 64 + kk * 32 + 32, cc * 64:cc * 64 + 64] for h in range(2)]
+                out[q, kk, cc] = jnp.concatenate(both, axis=1).reshape(8, 4, 128).astype(BF16)
+
+        @pl.loop(0, 8)
+        def _(i):
+            @pl.when(is_me(i))
+            def _():
+                pltpu.make_async_copy(out.at[q, k, c], mid2.at[q, me], c1r.at[q, me]).start()
+
+            @pl.when(jnp.logical_not(is_me(i)))
+            def _():
+                back_xy(q, i).start()
+
+    def back_z(j):
+        zz = lax.rem(z + hop(j), NZ)
+        at = NZ - 1 - j
+        return pltpu.make_async_remote_copy(
+            src_ref=mid2.at[at // 8, :, lax.rem(at, 8)], dst_ref=back.at[z], send_sem=c2s.at[j],
+            recv_sem=c2r.at[j], device_id=dev(y, zz, k, c), device_id_type=MESH)
+
+    def middle_arrived(q):
+        @pl.loop(0, 8)
+        def _(i):
+            pltpu.make_async_copy(mid2.at[q, i], mid2.at[q, i], c1r.at[q, i]).wait()
+
+    forward(0)
+    forward(1)
+    middle_arrived(0)
+
     @pl.loop(0, 8)
     def _(i):
-        @pl.when(is_me(i))
-        def _():
-            pltpu.make_async_copy(out.at[k, c], mid2.at[me], c1r.at[me]).start()
-
-        @pl.when(jnp.logical_not(is_me(i)))
-        def _():
-            back_xy(i).start()
+        back_z(NZ - 1 - i).start()
 
     @pl.loop(0, 8)
     def _(i):
@@ -358,20 +389,12 @@
         want = jnp.sum(jnp.where(sub == h * 4 + (lane & 3), full, 0.0), axis=0, keepdims=True)
         wants.append(want.astype(jnp.int32))
 
-    @pl.loop(0, 8)
-    def _(i):
-        pltpu.make_async_copy(mid2.at[i], mid2.at[i], c1r.at[i]).wait()
-
-    def back_z(i):
-        zz = lax.rem(z + i, NZ)
-        return pltpu.make_async_remote_copy(
-            src_ref=mid2.at[:, zz], dst_ref=back.at[z], send_sem=c2s.at[i], recv_sem=c2r.at[i],
-            device_id=dev(y, zz, k, c), device_id_type=MESH)
-
-    @pl.loop(1, NZ)
-    def _(i):
-        back_z(i).start()
-    own_back = pltpu.make_async_copy(mid2.at[:, z], back.at[z], c2r.at[0])
+    middle_arrived(1)
+
+    @pl.loop(8, NZ - 1)
+    def _(i):
+        back_z(NZ - 1 - i).start()
+    own_back = pltpu.make_async_copy(mid2.at[1, :, 7], back.at[z], c2r.at[0])
     own_back.start()
     for h in range(2):
         placing[h] = onehot(iota((1024, 512), 0) == wants[h])
@@ -391,7 +414,8 @@
         @pl.when(jnp.logical_not(is_me(i)))
         def _():
             pos_on(i).wait_send()
-            back_xy(i).wait_send()
+            back_xy(0, i).wait_send()
+            back_xy(1, i).wait_send()
             for g in range(8):
                 on(g, i).wait_send()
     own_back.wait()
@@ -420,9 +444,9 @@
             V((4, 256, 256), BF16),
             V((NZ, 2, 16, 128), BF16), V((NZ, 1, 128), I32), V((NZ, 1, 128), I32), V((8, NZ, 1, 128), I32),
             V((NZ, 2, 16, 128), BF16), V((NZ, 8, 16, 128), BF16), V((1024, 128), jnp.float32),
-            V((2, 4, NZ, 4, 128), BF16), V((8, NZ, 4, 128), BF16),
+            V((2, 2, 4, 8, 4, 128), BF16), V((2, 8, 8, 4, 128), BF16),
             sems(10), sems(NZ), sems(NZ), sems(NZ), sems(NZ), sems(8, 8), sems(8, 8),
-            sems(4, 4), sems(4, 4), sems(4, 4), sems(4, 4), sems(8), sems(8), sems(8), sems(8), sems(NZ), sems(NZ),
+            sems(4, 4), sems(4, 4), sems(4, 4), sems(4, 4), sems(8), sems(8), sems(2, 8), sems(2, 8), sems(NZ), sems(NZ),
             V((NZ, 8, 4, 128), BF16), V((2, 1024, 512), BF16),
         ],
         compiler_params=pltpu.CompilerParams(collective_id=0, has_side_effects=True,

time: 70.5 us -> 63.9 us (0.906)
  Pallas kernels: 68.5 us -> 62 us
    pallas_call x1, Pallas kernels: 68.5 us -> 62 us  [shards(): pl.pallas_call(layer_kernel, out_shape=S((64, 1024), BF16), in_specs=[ANY...]
where the time goes in v3:
time: 63.9 us; the launch traced here: 63.5 us
  Pallas kernels  62 us (97%)
  local copies, waits for them, and re-layouts  1.57 us (2%)
    pallas_call x1, Pallas kernels, shards(): pl.pallas_call(layer_kernel, out_shape=S((64, 1024), BF16), in_specs=[ANY...  62 us
    unnamed x1, local copies, waits for them, and re-layouts  1.57 us

profile of v3, /device:TPU:6, one launch (start us, length us, event | category | flops | bytes accessed | tf_op | source)
XLA Modules:
  0.0 63.5 jit_solution(14008980940702380205)
XLA Ops:
  0.0 62.0 %layer.1 = bf16[64,1024]{1,0:T(8,128)(2,1)} custom-call(bf16[3072,128]{1,0:T(8,128)(2,1)} %raw_h.1, s32[24,128]{1,0:T(8,128)} %bitcast.9, s32[1,2048]{1,0:T(1,128)} %hilbert_h.1, s32[8,128]{1,0:T(8,128)} %bitcast.10, s32[1,128]{1,0:T(1,128)} %bitcast.11, bf16[128,256]{1,0:T(8,128)(2,1)} %pool_h.1, bf16[3,64,256]{2,1,0:T(8,128)(2,1)} %bitcast.7, ...), custom_call_target="tpu_custom_call" | custom-call | tf_op jit(solution)/shard_map/layer/pallas_call | solution.py:436
  62.0 1.6 %copy.12 = bf16[1024,64]{0,1:T(8,128)(2,1)} copy(bf16[1024,64]{0,1:T(8,128)(2,1)} %bitcast.6) | data formatting | bytes 262144

commit v4 on v3

--- a/solution.py
+++ b/solution.py
@@ -65,25 +65,25 @@
     def hello(d):
         pl.semaphore_signal(barrier, inc=1, device_id=d, device_id_type=MESH)
 
-    hello(dev(y, z, 1 - k, c))
-    for i in range(1, 4):
-        hello(dev(y, z, k, lax.rem(c + i, 4)))
-
-    @pl.loop(1, NZ)
-    def _(i):
-        hello(dev(y, lax.rem(z + i, NZ), k, c))
-
-    @pl.loop(0, 8)
-    def _(i):
-        @pl.when(jnp.logical_not(on_diag & (i == me)))
-        def _():
-            hello(dev(i // 2, z, lax.rem(i, 2), y))
-
     loads = [pltpu.make_async_copy(a, b, lsem.at[i]) for i, (a, b) in enumerate((
         (hilbert_h, hilbert), (zpos_h, zpos), (ids_h, ids), (raw_h, raw), (counts_h, counts), (pool_h, pool),
         (qkv_h, wq.at[c]), (proj_h, wp.at[c]), (fc1_h, w1.at[c]), (fc2_h, w2.at[c])))]
     for load in loads:
         load.start()
+
+    hello(dev(y, z, 1 - k, c))
+    for i in range(1, 4):
+        hello(dev(y, z, k, lax.rem(c + i, 4)))
+
+    @pl.loop(1, NZ)
+    def _(i):
+        hello(dev(y, lax.rem(z + i, NZ), k, c))
+
+    @pl.loop(0, 8)
+    def _(i):
+        @pl.when(jnp.logical_not(on_diag & (i == me)))
+        def _():
+            hello(dev(i // 2, z, lax.rem(i, 2), y))
 
     loads[0].wait()
     target = hilbert[...]
@@ -168,7 +168,7 @@
     def on(g, i):
         kk, cc = lax.rem(i, 2), i // 2
         return pltpu.make_async_remote_copy(
-            src_ref=mid.at[2 * g:2 * g + 2, kk], dst_ref=rows.at[2 * g:2 * g + 2, me],
+            src_ref=mid.at[4 * g:4 * g + 4, kk], dst_ref=rows.at[4 * g:4 * g + 4, me],
             send_sem=s3.at[g, i], recv_sem=r3.at[g, me],
             device_id=dev(c, z, kk, cc), device_id_type=MESH)
 
@@ -177,7 +177,7 @@
         def _(i):
             @pl.when(is_me(i))
             def _():
-                pltpu.make_async_copy(mid.at[2 * g:2 * g + 2, k], rows.at[2 * g:2 * g + 2, me],
+                pltpu.make_async_copy(mid.at[4 * g:4 * g + 4, k], rows.at[4 * g:4 * g + 4, me],
                                       r3.at[g, me]).start()
 
             @pl.when(jnp.logical_not(is_me(i)))
@@ -187,7 +187,7 @@
     def on_arrived(g):
         @pl.loop(0, 8)
         def _(i):
-            block = rows.at[2 * g:2 * g + 2, i]
+            block = rows.at[4 * g:4 * g + 4, i]
             pltpu.make_async_copy(block, block, r3.at[g, i]).wait()
 
     loads[1].wait()
@@ -236,15 +236,15 @@
 
     def gather_group(g):
         on_arrived(g)
-        sel = onehot(iota((1024, 256), 0) == order[:, g * 256:(g + 1) * 256])
-        piece = dot(sel, rows[2 * g:2 * g + 2].reshape(256, 128))
+        sel = onehot(iota((1024, 512), 0) == order[:, g * 512:(g + 1) * 512])
+        piece = dot(sel, rows[4 * g:4 * g + 4].reshape(512, 128))
         if g == 0:
             acc[...] = piece
         else:
             acc[...] += piece
 
-    for g in range(8):
-        for j in (2 * g, 2 * g + 1):
+    for g in range(4):
+        for j in range(4 * g, 4 * g + 4):
             pltpu.make_async_copy(mid.at[j], mid.at[j], r2.at[j]).wait()
         on_start(g)
         if g == 0:
@@ -257,7 +257,7 @@
     for i in range(1, 4):
         weight_x(0, i).wait_recv()
         weight_core(0, i).start()
-    for g in range(8):
+    for g in range(4):
         gather_group(g)
 
     @pl.loop(0, NZ)
@@ -416,7 +416,7 @@
             pos_on(i).wait_send()
             back_xy(0, i).wait_send()
             back_xy(1, i).wait_send()
-            for g in range(8):
+            for g in range(4):
                 on(g, i).wait_send()
     own_back.wait()
 
@@ -445,7 +445,7 @@
             V((NZ, 2, 16, 128), BF16), V((NZ, 1, 128), I32), V((NZ, 1, 128), I32), V((8, NZ, 1, 128), I32),
             V((NZ, 2, 16, 128), BF16), V((NZ, 8, 16, 128), BF16), V((1024, 128), jnp.float32),
             V((2, 2, 4, 8, 4, 128), BF16), V((2, 8, 8, 4, 128), BF16),
-            sems(10), sems(NZ), sems(NZ), sems(NZ), sems(NZ), sems(8, 8), sems(8, 8),
+            sems(10), sems(NZ), sems(NZ), sems(NZ), sems(NZ), sems(4, 8), sems(4, 8),
             sems(4, 4), sems(4, 4), sems(4, 4), sems(4, 4), sems(8), sems(8), sems(2, 8), sems(2, 8), sems(NZ), sems(NZ),
             V((NZ, 8, 4, 128), BF16), V((2, 1024, 512), BF16),
         ],

time: 63.9 us -> 63.3 us (level); the launches traced: 63.5 us -> 62.3 us
  Pallas kernels: 62 us -> 60.7 us
    pallas_call x1, Pallas kernels: 62 us -> 60.7 us  [shards(): pl.pallas_call(layer_kernel, out_shape=S((64, 1024), BF16), in_specs=[ANY...]
where the time goes in v4:
time: 63.3 us; the launch traced here: 62.3 us
  Pallas kernels  60.7 us (96%)
  local copies, waits for them, and re-layouts  1.57 us (2%)
    pallas_call x1, Pallas kernels, shards(): pl.pallas_call(layer_kernel, out_shape=S((64, 1024), BF16), in_specs=[ANY...  60.7 us
    unnamed x1, local copies, waits for them, and re-layouts  1.57 us

profile of v4, /device:TPU:6, one launch (start us, length us, event | category | flops | bytes accessed | tf_op | source)
XLA Modules:
  0.0 62.3 jit_solution(15867940101085917577)
XLA Ops:
  0.0 60.7 %layer.1 = bf16[64,1024]{1,0:T(8,128)(2,1)} custom-call(bf16[3072,128]{1,0:T(8,128)(2,1)} %raw_h.1, s32[24,128]{1,0:T(8,128)} %bitcast.9, s32[1,2048]{1,0:T(1,128)} %hilbert_h.1, s32[8,128]{1,0:T(8,128)} %bitcast.10, s32[1,128]{1,0:T(1,128)} %bitcast.11, bf16[128,256]{1,0:T(8,128)(2,1)} %pool_h.1, bf16[3,64,256]{2,1,0:T(8,128)(2,1)} %bitcast.7, ...), custom_call_target="tpu_custom_call" | custom-call | tf_op jit(solution)/shard_map/layer/pallas_call | solution.py:436
  60.7 1.6 %copy.12 = bf16[1024,64]{0,1:T(8,128)(2,1)} copy(bf16[1024,64]{0,1:T(8,128)(2,1)} %bitcast.6) | data formatting | bytes 262144

commit v5 on v4

--- a/solution.py
+++ b/solution.py
@@ -251,14 +251,14 @@
             @pl.loop(1, NZ)
             def _(j):
                 pos_z(j).start()
-    for a in range(1, 4):
-        for i in range(1, 4):
-            weight_x(a, i).start()
     for i in range(1, 4):
         weight_x(0, i).wait_recv()
         weight_core(0, i).start()
     for g in range(4):
         gather_group(g)
+    for a in range(1, 4):
+        for i in range(1, 4):
+            weight_x(a, i).start()
 
     @pl.loop(0, NZ)
     def _(j):
@@ -309,7 +309,7 @@
     scores = score(0)
     for h in range(16):
         later = score(h + 1) if h < 15 else None
-        if h == 12:
+        if h == 14:
             for a in range(1, 4):
                 for i in range(1, 4):
                     weight_x(a, i).wait_recv()

time: 63.3 us -> 64.8 us (1.024)
  Pallas kernels: 60.7 us -> 62.3 us
    pallas_call x1, Pallas kernels: 60.7 us -> 62.3 us  [shards(): pl.pallas_call(layer_kernel, out_shape=S((64, 1024), BF16), in_specs=[ANY...]
where the time goes in v5:
time: 64.8 us; the launch traced here: 63.9 us
  Pallas kernels  62.3 us (96%)
  local copies, waits for them, and re-layouts  1.57 us (2%)
    pallas_call x1, Pallas kernels, shards(): pl.pallas_call(layer_kernel, out_shape=S((64, 1024), BF16), in_specs=[ANY...  62.3 us
    unnamed x1, local copies, waits for them, and re-layouts  1.57 us

profile of v5, /device:TPU:6, one launch (start us, length us, event | category | flops | bytes accessed | tf_op | source)
XLA Modules:
  0.0 63.9 jit_solution(15734820752082207945)
XLA Ops:
  0.0 62.3 %layer.1 = bf16[64,1024]{1,0:T(8,128)(2,1)} custom-call(bf16[3072,128]{1,0:T(8,128)(2,1)} %raw_h.1, s32[24,128]{1,0:T(8,128)} %bitcast.9, s32[1,2048]{1,0:T(1,128)} %hilbert_h.1, s32[8,128]{1,0:T(8,128)} %bitcast.10, s32[1,128]{1,0:T(1,128)} %bitcast.11, bf16[128,256]{1,0:T(8,128)(2,1)} %pool_h.1, bf16[3,64,256]{2,1,0:T(8,128)(2,1)} %bitcast.7, ...), custom_call_target="tpu_custom_call" | custom-call | tf_op jit(solution)/shard_map/layer/pallas_call | solution.py:436
  62.3 1.6 %copy.12 = bf16[1024,64]{0,1:T(8,128)(2,1)} copy(bf16[1024,64]{0,1:T(8,128)(2,1)} %bitcast.6) | data formatting | bytes 262144
